TPU v7x, 32 devices: a whole 2x2x4 slice. The times are simulated.
32 devices in a mesh: dom: 8 (over y, x, core), sub: 4 (over z).
Axes of the slice: x: 2, y: 2, z: 4, core: 2. Of those that a mesh axis runs over, the one named last changes fastest.
Arguments:
- features: float32 [16384, 602], P(('dom', 'sub')), may hold values from -6 to 6
- hub_features: float32 [256, 602], replicated, may hold values from -6 to 6
- low_lists: int32 [8192, 4], P(('dom', 'sub')), may hold values from 0 to 1791
- low_masks: int32 [8192, 4], P(('dom', 'sub')), may hold values 0 or 1
- high_lists: int32 [8192, 32], P(('dom', 'sub')), may hold values from 0 to 1791
- high_masks: int32 [8192, 32], P(('dom', 'sub')), may hold values 0 or 1
- hub_lists: int32 [32, 256, 16], P(('dom', 'sub')), may hold values from 0 to 1791
- hub_masks: int32 [32, 256, 16], P(('dom', 'sub')), may hold values 0 or 1
- send_rows: int32 [32, 32, 32], P(('dom', 'sub')), may hold values from 0 to 511
- labels: int32 [16384], P(('dom', 'sub')), may hold values from 0 to 40
- train_mask: int32 [16384], P(('dom', 'sub')), may hold values from 0 to 1
- stale_rows: float32 [2, 32768, 256], P(None, ('dom', 'sub')), may hold values from -4 to 4
- weight_one: float32 [1204, 256], replicated, may hold values from -2 to 2
- weight_two: float32 [512, 256], replicated, may hold values from -2 to 2
- weight_three: float32 [512, 41], replicated, may hold values from -2 to 2
- biases: float32 [553], replicated, may hold values from -1.5 to 1.5
- mean_one: float32 [1204, 256], replicated, may hold values from -0.0004272461 to 0.0004272461
- mean_two: float32 [512, 256], replicated, may hold values from -0.0004272461 to 0.0004272461
- mean_three: float32 [512, 41], replicated, may hold values from -0.0004272461 to 0.0004272461
- mean_biases: float32 [553], replicated, may hold values from -0.0017089844 to 0.0017089844
- square_one: float32 [1204, 256], replicated, may hold values from 8.676018e-10 to 3.4704073e-09
- square_two: float32 [512, 256], replicated, may hold values from 8.676018e-10 to 3.4704073e-09
- square_three: float32 [512, 41], replicated, may hold values from 8.676018e-10 to 3.4704073e-09
- square_biases: float32 [553], replicated, may hold values from 1.3881629e-08 to 5.5526517e-08
Outputs:
- grad_norm: float32 [], replicated
- loss_sum: float32 [], replicated
- train_count: float32 [], replicated
- new_one: float32 [1204, 256], replicated
- new_two: float32 [512, 256], replicated
- new_three: float32 [512, 41], replicated
- new_biases: float32 [553], replicated
- moment_one: float32 [1204, 256], replicated
- moment_two: float32 [512, 256], replicated
- moment_three: float32 [512, 41], replicated
- moment_biases: float32 [553], replicated
- second_one: float32 [1204, 256], replicated
- second_two: float32 [512, 256], replicated
- second_three: float32 [512, 41], replicated
- second_biases: float32 [553], replicated
- copy_one: bfloat16 [1204, 256], replicated
- copy_two: bfloat16 [512, 256], replicated
- copy_three: bfloat16 [512, 41], replicated
- copy_biases: bfloat16 [553], replicated
- new_stale: float32 [2, 32768, 256], P(None, ('dom', 'sub'))
Inputs may be any that keep to these rules, and one draw needn't show every extreme that they name: `send_rows`: rows of the sending device's own nodes.
All inputs are finite; a program needn't handle non-finite values. No bound on the sum of `low_masks` or of `high_masks` or of `hub_masks` on one device may be relied on, other than what follows from the above.
Results may differ from a plain program's by a relative error of at most 0.001.
Values sent between devices are 32-bit elements; how exact they have to be, the bound alone decides.
A program may use at most 128 MiB of HBM per device.

v0:
```python
import jax
import jax.numpy as jnp
from jax import lax
from jax.sharding import PartitionSpec as P

STEP = 5


precise = lax.Precision.HIGHEST
keep_share = 0.95
smooth = 0.1
clip_level = 0.02
learn_rate = 0.03
weight_decay = 0.01
beta_first = 0.5
beta_second = 0.5
epsilon = 1e-08


def matmul_exact(left, right):
    return jnp.dot(left, right, precision=precise, preferred_element_type=jnp.float32)


def contract_rows(left, right):
    return lax.dot_general(
        left, right, (((0,), (0,)), ((), ())), precision=precise, preferred_element_type=jnp.float32
    )


def against_weight(grad_rows, weight):
    return lax.dot_general(
        grad_rows,
        weight,
        (((1,), (1,)), ((), ())),
        precision=precise,
        preferred_element_type=jnp.float32,
    )


def gelu_smooth(values):
    return jax.nn.gelu(values, approximate=True)


def gelu_back(pre_values, grad_values):
    unused, pull = jax.vjp(gelu_smooth, pre_values)
    return pull(grad_values)[0]


def mean_weights(selector):
    weights = selector.astype(jnp.float32)
    return weights / jnp.maximum(jnp.sum(weights, axis=1), 1.0)[:, None]


def gather_mean(lookup, indices, scaled):
    row_count = indices.shape[0]
    block_size = min(256, row_count)
    block_count = row_count // block_size

    def one_block(inputs):
        block_index, block_weights = inputs
        return jnp.einsum("nkf,nk->nf", lookup[block_index], block_weights, precision=precise)

    summed = lax.map(
        one_block,
        (indices.reshape(block_count, block_size, -1), scaled.reshape(block_count, block_size, -1)),
    )
    return summed.reshape(row_count, lookup.shape[1])


def send_forward(blocks):
    return lax.all_to_all(blocks, ("dom", "sub"), split_axis=0, concat_axis=0, tiled=True)


def send_back(blocks):
    return lax.all_to_all(blocks, ("dom", "sub"), split_axis=0, concat_axis=0, tiled=True)


def local(
    features,
    hub_features,
    low_lists,
    low_masks,
    high_lists,
    high_masks,
    hub_lists,
    hub_masks,
    send_rows,
    labels,
    train_mask,
    stale_rows,
    weight_one,
    weight_two,
    weight_three,
    biases,
    mean_one,
    mean_two,
    mean_three,
    mean_biases,
    square_one,
    square_two,
    square_three,
    square_biases,
):
    node_count = features.shape[0]
    low_rows = low_lists.shape[0]
    send_local = send_rows[0]
    peer_count = send_local.shape[0]
    halo_count = stale_rows.shape[1]
    hub_index = hub_lists[0]
    hub_weights = hub_masks[0].astype(jnp.float32)
    low_scaled = mean_weights(low_masks)
    high_scaled = mean_weights(high_masks)
    train_weights = train_mask.astype(jnp.float32)
    layer_weights = (weight_one, weight_two, weight_three)
    hidden = weight_one.shape[1]
    bias_parts = (biases[:hidden], biases[hidden : 2 * hidden], biases[2 * hidden :])
    send_flat = send_local.reshape(-1)
    owned = features
    hub_rows = hub_features
    renewed = []
    stored = []
    hub_count = None
    train_count = None
    node_pre = None
    for layer_index in range(3):
        feature_width = owned.shape[1]
        outgoing = owned[send_flat].reshape(peer_count, -1, feature_width)
        fresh_rows = send_forward(outgoing).reshape(halo_count, feature_width)
        if layer_index == 0:
            halo_rows = fresh_rows
        else:
            halo_rows = keep_share * stale_rows[layer_index - 1] + (1.0 - keep_share) * fresh_rows
            renewed.append(halo_rows)
        lookup = jnp.concatenate([owned, halo_rows, hub_rows], axis=0)
        mean_rows = jnp.concatenate(
            [
                gather_mean(lookup, low_lists, low_scaled),
                gather_mean(lookup, high_lists, high_scaled),
            ],
            axis=0,
        )
        node_in = jnp.concatenate([owned, mean_rows], axis=1)
        node_pre = matmul_exact(node_in, layer_weights[layer_index]) + bias_parts[layer_index]
        hub_in = None
        hub_pre = None
        if layer_index < 2:
            hub_partial = jnp.einsum(
                "hkf,hk->hf", lookup[hub_index], hub_weights, precision=precise
            )
            if layer_index == 0:
                hub_sum, hub_count, train_count = lax.psum(
                    (hub_partial, jnp.sum(hub_weights, axis=1), jnp.sum(train_weights)),
                    ("dom", "sub"),
                )
            else:
                hub_sum = lax.psum(hub_partial, ("dom", "sub"))
            hub_in = jnp.concatenate([hub_rows, hub_sum / hub_count[:, None]], axis=1)
            hub_pre = matmul_exact(hub_in, layer_weights[layer_index]) + bias_parts[layer_index]
            owned = gelu_smooth(node_pre)
            hub_rows = gelu_smooth(hub_pre)
        stored.append((node_in, node_pre, hub_in, hub_pre))
    log_probs = jax.nn.log_softmax(node_pre, axis=1)
    onehot = (labels[:, None] == jnp.arange(node_pre.shape[1], dtype=jnp.int32)[None, :]).astype(
        jnp.float32
    )
    target = (1.0 - smooth) * onehot + smooth / node_pre.shape[1]
    loss_local = jnp.sum(-jnp.sum(target * log_probs, axis=1) * train_weights)
    grad_pre = (jnp.exp(log_probs) - target) * train_weights[:, None] / train_count
    hub_grad_pre = None
    weight_grads = [None, None, None]
    bias_grads = [None, None, None]
    hub_weight_grads = [None, None, None]
    hub_bias_grads = [None, None, None]
    for layer_index in (2, 1, 0):
        node_in, unused_pre, hub_in, unused_hub = stored[layer_index]
        weight = layer_weights[layer_index]
        weight_grads[layer_index] = contract_rows(node_in, grad_pre)
        bias_grads[layer_index] = jnp.sum(grad_pre, axis=0)
        if hub_grad_pre is not None:
            hub_weight_grads[layer_index] = contract_rows(hub_in, hub_grad_pre)
            hub_bias_grads[layer_index] = jnp.sum(hub_grad_pre, axis=0)
        else:
            hub_weight_grads[layer_index] = jnp.zeros_like(weight)
            hub_bias_grads[layer_index] = jnp.zeros_like(bias_parts[layer_index])
        if layer_index > 0:
            feature_width = node_in.shape[1] // 2
            node_back = against_weight(grad_pre, weight)
            self_grad = node_back[:, :feature_width]
            mean_grad = node_back[:, feature_width:]
            table_grad = jnp.zeros(
                (node_count + halo_count + hub_rows.shape[0], feature_width), jnp.float32
            )
            low_terms = mean_grad[:low_rows, None, :] * low_scaled[:, :, None]
            high_terms = mean_grad[low_rows:, None, :] * high_scaled[:, :, None]
            table_grad = table_grad.at[low_lists.reshape(-1)].add(
                low_terms.reshape(-1, feature_width)
            )
            table_grad = table_grad.at[high_lists.reshape(-1)].add(
                high_terms.reshape(-1, feature_width)
            )
            hub_self = None
            if hub_grad_pre is not None:
                hub_back = against_weight(hub_grad_pre, weight)
                hub_self = hub_back[:, :feature_width]
                hub_mean_grad = hub_back[:, feature_width:] / hub_count[:, None]
                hub_terms = hub_mean_grad[:, None, :] * hub_weights[:, :, None]
                table_grad = table_grad.at[hub_index.reshape(-1)].add(
                    hub_terms.reshape(-1, feature_width)
                )
            own_grad = self_grad + table_grad[:node_count]
            halo_grad = table_grad[node_count : node_count + halo_count] * (1.0 - keep_share)
            returned = send_back(halo_grad.reshape(peer_count, -1, feature_width))
            own_grad = own_grad.at[send_flat].add(returned.reshape(-1, feature_width))
            hub_total = lax.psum(table_grad[node_count + halo_count :], ("dom", "sub"))
            if hub_self is not None:
                hub_total = hub_total + hub_self
            previous = stored[layer_index - 1]
            grad_pre = gelu_back(previous[1], own_grad)
            hub_grad_pre = gelu_back(previous[3], hub_total)
    summed_one, summed_two, summed_three, summed_bias, loss_sum = lax.psum(
        (
            weight_grads[0],
            weight_grads[1],
            weight_grads[2],
            jnp.concatenate(bias_grads),
            loss_local,
        ),
        ("dom", "sub"),
    )
    gradients = (
        summed_one + hub_weight_grads[0],
        summed_two + hub_weight_grads[1],
        summed_three,
        summed_bias + jnp.concatenate(hub_bias_grads),
    )
    grad_norm = jnp.sqrt(sum((jnp.sum(grad * grad) for grad in gradients)))
    factor = jnp.minimum(1.0, clip_level / (grad_norm + 1e-06))
    params = (weight_one, weight_two, weight_three, biases)
    firsts = (mean_one, mean_two, mean_three, mean_biases)
    seconds = (square_one, square_two, square_three, square_biases)
    new_params, new_firsts, new_seconds = ([], [], [])
    for weight, grad, first, second in zip(params, gradients, firsts, seconds):
        clipped = grad * factor
        moment = beta_first * first + (1.0 - beta_first) * clipped
        squared = beta_second * second + (1.0 - beta_second) * clipped * clipped
        unbiased = moment / (1.0 - beta_first**STEP)
        scaled = squared / (1.0 - beta_second**STEP)
        new_params.append(
            weight - learn_rate * (unbiased / (jnp.sqrt(scaled) + epsilon) + weight_decay * weight)
        )
        new_firsts.append(moment)
        new_seconds.append(squared)
    return (
        grad_norm,
        loss_sum,
        train_count,
        new_params[0],
        new_params[1],
        new_params[2],
        new_params[3],
        new_firsts[0],
        new_firsts[1],
        new_firsts[2],
        new_firsts[3],
        new_seconds[0],
        new_seconds[1],
        new_seconds[2],
        new_seconds[3],
        new_params[0].astype(jnp.bfloat16),
        new_params[1].astype(jnp.bfloat16),
        new_params[2].astype(jnp.bfloat16),
        new_params[3].astype(jnp.bfloat16),
        jnp.stack(renewed),
    )


def solution(mesh):
    in_specs = (
        P(("dom", "sub"), None),
        P(),
        P(("dom", "sub"), None),
        P(("dom", "sub"), None),
        P(("dom", "sub"), None),
        P(("dom", "sub"), None),
        P(("dom", "sub"), None, None),
        P(("dom", "sub"), None, None),
        P(("dom", "sub"), None, None),
        P(("dom", "sub")),
        P(("dom", "sub")),
        P(None, ("dom", "sub"), None),
        P(),
        P(),
        P(),
        P(),
        P(),
        P(),
        P(),
        P(),
        P(),
        P(),
        P(),
        P(),
    )
    out_specs = (
        P(),
        P(),
        P(),
        P(),
        P(),
        P(),
        P(),
        P(),
        P(),
        P(),
        P(),
        P(),
        P(),
        P(),
        P(),
        P(),
        P(),
        P(),
        P(),
        P(None, ("dom", "sub"), None),
    )
    return jax.shard_map(local, mesh=mesh, in_specs=in_specs, out_specs=out_specs, check_vma=False)
```

profile of v0, /device:TPU:0, one launch (start us, length us, event | category | flops | bytes accessed | tf_op | source)
XLA Modules:
  0.0 1098.2 jit_solution(6254002579975791371)
XLA Ops:
  10.3 5.2 gather_fusion
  15.5 7.4 all-to-all-start
  25.3 56.6 %all-to-all-done = f32[32,32,602]{2,1,0:T(8,128)} async-done(((f32[32,32,602]{2,1,0:T(8,128)}), f32[32,32,602]{2,1,0:T(8,128)}, u32[]{:S(2)}, u32[]{:S(2)}) %all-to-all-start) | async-done | bytes 2465824 | tf_op jit(solution)/shard_map/all_to_all | solution.py:71
  81.9 4.2 pad_maximum_fusion
  86.0 38.9 %gather_fusion.2 = f32[8192,602]{1,0:T(8,128)} fusion(f32[1792,602]{1,0:T(8,128)} %pad_maximum_fusion, s32[8192]{0:T(1024)S(1)} %broadcast_clamp_fusion), kind=kCustom, calls=%fused_computation.2 | custom fusion | bytes 39485440 | tf_op jit(solution)/shard_map/while/body/eval_jaxpr/gather | solution.py:61
  125.0 10.8 multiply_reduce_fusion
  136.9 7.8 gather_fusion.1
  144.7 2.8 reshape.346
  151.3 7.2 multiply_multiply_fusion.7
  158.5 4.7 gather_fusion.3
  163.2 4.6 all-to-all-start.1
  168.4 21.2 %gather_fusion.4 = f32[4096,602]{1,0:T(8,128)} fusion(f32[1792,602]{1,0:T(8,128)} %pad_maximum_fusion, s32[4096]{0:T(1024)S(1)} %broadcast_clamp_fusion.1), kind=kCustom, calls=%fused_computation.4 | custom fusion | bytes 19742720 | tf_op jit(solution)/shard_map/gather | solution.py:148
  189.6 6.2 multiply_reduce_fusion.1
  199.8 40.8 %all-reduce.1 = (f32[256]{0:T(256)S(1)}, f32[]{:T(128)}) all-reduce(f32[256]{0:T(256)S(1)} %convert_reduce_fusion.3, f32[]{:T(128)} %convert_reduce_fusion.2), channel_id=1, replica_groups=mesh['dom'=8,'sub'=4] {'dom','sub'}, use_global_device_ids=true, to_apply=%region_4.5 | all-reduce | flops 257 | bytes 2056 | tf_op jit(solution)/shard_map/psum | solution.py:151
  240.6 85.6 %all-reduce.8.cloned.1.call-done = f32[256,602]{0,1:T(8,128)} async-done(((f32[256,602]{0,1:T(8,128)}), f32[256,602]{0,1:T(8,128)}) %all-reduce.8.cloned.1.call-update) | async-done | bytes 616464 | tf_op jit(solution)/shard_map/psum | solution.py:151
  328.2 4.6 multiply_multiply_fusion.13
  335.3 31.4 %gather_fusion.6 = f32[8192,256]{1,0:T(8,128)} fusion(f32[1792,256]{1,0:T(8,128)S(1)} %pad_maximum_fusion.2, s32[8192]{0:T(1024)S(1)} %broadcast_clamp_fusion), kind=kCustom, calls=%fused_computation.6 | custom fusion | bytes 16809984 | tf_op jit(solution)/shard_map/while/body/eval_jaxpr/gather | solution.py:61
  366.8 4.7 gather_fusion.5
  374.0 7.0 fusion.75
  385.0 4.7 gather_fusion.7
  389.7 4.4 all-to-all-start.2
  395.1 16.1 %gather_fusion.8 = f32[4096,256]{1,0:T(8,128)} fusion(f32[1792,256]{1,0:T(8,128)S(1)} %pad_maximum_fusion.2, s32[4096]{0:T(1024)S(1)} %broadcast_clamp_fusion.1), kind=kCustom, calls=%fused_computation.8 | custom fusion | bytes 8404992 | tf_op jit(solution)/shard_map/gather | solution.py:148
  411.2 4.7 fusion.76
  417.3 125.7 %all-reduce.10.cloned.1.call-done = f32[256,256]{1,0:T(8,128)} async-done(((f32[256,256]{1,0:T(8,128)}), f32[256,256]{1,0:T(8,128)}) %all-reduce.10.cloned.1.call-update) | async-done | bytes 262160 | tf_op jit(solution)/shard_map/psum | solution.py:156
  548.8 31.4 %gather_fusion.10 = f32[8192,256]{1,0:T(8,128)} fusion(f32[1792,256]{1,0:T(8,128)S(1)} %pad_maximum_fusion.3, s32[8192]{0:T(1024)S(1)} %broadcast_clamp_fusion), kind=kCustom, calls=%fused_computation.10 | custom fusion | bytes 16809984 | tf_op jit(solution)/shard_map/while/body/eval_jaxpr/gather | solution.py:61
  580.3 4.7 gather_fusion.9
  584.9 7.4 fusion.78
  600.6 3.9 bitcast_multiply_fusion.1
  604.5 7.5 scatter_custom_fusion
  612.0 45.3 %scatter_fusion = f32[1792,256]{1,0:T(8,128)S(1)} fusion(f32[1792,256]{1,0:T(8,128)S(1)} %scatter_custom_fusion, s32[8192]{0:T(1024)S(1)} %bitcast.97, f32[8192,256]{1,0:T(8,128)} %bitcast_multiply_fusion.1), kind=kCustom, calls=%fused_computation.12 | custom fusion | flops 2097152 | bytes 25198592 | tf_op jit(solution)/shard_map/scatter-add | solution.py:198
  658.4 3.8 all-to-all-start.3
  665.9 130.8 %all-reduce.12.cloned.1.call-done = f32[256,256]{1,0:T(8,128)} async-done(((f32[256,256]{1,0:T(8,128)}), f32[256,256]{1,0:T(8,128)}) %all-reduce.12.cloned.1.call-update) | async-done | bytes 262160 | tf_op jit(solution)/shard_map/psum | solution.py:214
  801.7 6.8 scatter_fusion.1
  810.5 4.0 bitcast_multiply_fusion
  816.1 7.5 scatter_custom_fusion.3
  823.6 45.3 %scatter_fusion.2 = f32[1792,256]{1,0:T(8,128)S(1)} fusion(f32[1792,256]{1,0:T(8,128)S(1)} %scatter_custom_fusion.3, s32[8192]{0:T(1024)S(1)} %bitcast.98, f32[8192,256]{1,0:T(8,128)} %bitcast_multiply_fusion), kind=kCustom, calls=%fused_computation.15 | custom fusion | flops 2097152 | bytes 25198592 | tf_op jit(solution)/shard_map/scatter-add | solution.py:198
  868.9 23.7 %scatter_fusion.3 = f32[1792,256]{1,0:T(8,128)S(1)} fusion(f32[1792,256]{1,0:T(8,128)S(1)} %scatter_fusion.2, s32[4096]{0:T(1024)S(1)} %bitcast.103, f32[4096,256]{1,0:T(8,128)} %bitcast_multiply_fusion.2), kind=kCustom, calls=%fused_computation.16 | custom fusion | flops 1048576 | bytes 12599296 | tf_op jit(solution)/shard_map/scatter-add | solution.py:207
  893.8 3.8 all-to-all-start.4
  897.7 3.3 fusion.10
  901.7 2.6 fusion.11
  904.4 18.2 %all-to-all-done.4 = f32[32,32,256]{2,1,0:T(8,128)} async-done(((f32[32,32,256]{2,1,0:T(8,128)}), f32[32,32,256]{2,1,0:T(8,128)}, u32[]{:S(2)}, u32[]{:S(2)}) %all-to-all-start.4) | async-done | bytes 1048608 | tf_op jit(solution)/shard_map/all_to_all | solution.py:75
  922.6 6.8 scatter_fusion.4
  931.0 4.2 fusion
  940.1 41.3 %all-reduce = (f32[553]{0:T(1024)S(1)}, f32[]{:T(128)}) all-reduce(f32[553]{0:T(1024)S(1)} %pad_maximum_fusion.10, f32[]{:T(128)} %multiply_reduce_fusion.8), channel_id=1, replica_groups=mesh['dom'=8,'sub'=4] {'dom','sub'}, use_global_device_ids=true, to_apply=%region_28.29 | all-reduce | flops 554 | bytes 4432 | tf_op jit(solution)/shard_map/psum | solution.py:220
  981.4 89.0 %all-reduce.14.cloned.1.call-done = (f32[1204,256]{1,0:T(8,128)}, f32[256,256]{1,0:T(8,128)}, f32[512,256]{1,0:T(8,128)}, f32[512,41]{0,1:T(8,128)}) async-done(((f32[1204,256]{1,0:T(8,128)}, f32[256,256]{1,0:T(8,128)}, f32[512,256]{1,0:T(8,128)}, f32[512,41]{0,1:T(8,128)}), (f32[1204,256]{1,0:T(8,128)}, f32[256,256]{1,0:T(8,128)}, f32[512,256]{1,0:T(8,128)}, ...) | async-done | bytes 2103312 | tf_op jit(solution)/shard_map/psum | solution.py:220
  1070.4 3.5 multiply_reduce_fusion.4
  1084.3 3.0 fusion.57
  1087.3 2.8 fusion.59
  (286 shorter events, 70.9 us)
Async XLA Ops:
  15.5 7.4 copy-start.9
  15.5 7.7 copy-start.52
  15.5 7.9 copy-start.49
  15.5 66.4 %all-to-all-start = ((f32[32,32,602]{2,1,0:T(8,128)}), f32[32,32,602]{2,1,0:T(8,128)}, u32[]{:S(2)}, u32[]{:S(2)}) async-start(f32[32,32,602]{2,1,0:T(8,128)} %bitcast.90), calls=%async_computation | async-start | bytes 5242880 | tf_op jit(solution)/shard_map/all_to_all | solution.py:71
  24.7 126.6 %copy-start.78 = (f32[256]{0:T(256)}, f32[256]{0:T(256)S(1)}, u32[]{:S(2)}) copy-start(f32[256]{0:T(256)S(1)} %get-tuple-element.154) | copy-start | bytes 3076
  151.3 7.2 copy-start.25
  158.5 224.6 %copy-start = (f32[512,256]{1,0:T(8,128)}, f32[512,256]{1,0:T(8,128)S(1)}, u32[]{:S(2)}) copy-start(f32[512,256]{1,0:T(8,128)S(1)} %get-tuple-element.157) | copy-start | bytes 1572868
  163.2 169.6 %all-to-all-start.1 = ((f32[32,32,256]{2,1,0:T(8,128)}), f32[32,32,256]{2,1,0:T(8,128)}, u32[]{:S(2)}, u32[]{:S(2)}) async-start(f32[32,32,256]{2,1,0:T(8,128)} %bitcast.5), calls=%async_computation.1 | async-start | bytes 2097152 | tf_op jit(solution)/shard_map/all_to_all | solution.py:71
  167.8 158.4 %all-reduce.8.cloned.1.call-start = ((), (), s32[]{:S(2)}) async-start(), calls=%async_computation.5 | async-start | bytes 1245184 | tf_op jit(solution)/shard_map/psum | solution.py:151
  198.0 175.9 %copy-start.35 = (f32[256,32,1]{1,2,0:T(1,128)}, f32[256,32,1]{1,2,0:T(1,128)S(1)}, u32[]{:S(2)}) copy-start(f32[256,32,1]{1,2,0:T(1,128)S(1)} %copy.73) | copy-start | bytes 98308
  198.2 182.8 %copy-start.53 = (f32[256,4,1]{1,2,0:T(1,128)}, f32[256,4,1]{1,2,0:T(1,128)S(1)}, u32[]{:S(2)}) copy-start(f32[256,4,1]{1,2,0:T(1,128)S(1)} %copy.71) | copy-start | bytes 12292
  240.6 302.4 %copy-start.74 = (f32[256]{0:T(256)}, f32[256]{0:T(256)S(1)}, u32[]{:S(2)}) copy-start(f32[256]{0:T(256)S(1)} %get-tuple-element.104) | copy-start | bytes 3076
  328.2 6.0 copy-start.6
  374.0 7.0 copy-start.38
  389.7 156.5 %all-to-all-start.2 = ((f32[32,32,256]{2,1,0:T(8,128)}), f32[32,32,256]{2,1,0:T(8,128)}, u32[]{:S(2)}, u32[]{:S(2)}) async-start(f32[32,32,256]{2,1,0:T(8,128)} %bitcast.93), calls=%async_computation.2 | async-start | bytes 2097152 | tf_op jit(solution)/shard_map/all_to_all | solution.py:71
  394.1 148.8 %all-reduce.10.cloned.1.call-start = ((), (), s32[]{:S(2)}) async-start(), calls=%async_computation.6 | async-start | bytes 524288 | tf_op jit(solution)/shard_map/psum | solution.py:156
  395.1 16.1 %copy-start.43 = (f32[256,16,1]{1,2,0:T(1,128)S(1)}, f32[256,16,1]{1,2,0:T(1,128)}, u32[]{:S(2)}) copy-start(f32[256,16,1]{1,2,0:T(1,128)} %copy.75) | copy-start | bytes 49156
  411.2 133.6 %copy-start.22 = (f32[256,256]{1,0:T(8,128)S(1)}, f32[256,256]{1,0:T(8,128)}, u32[]{:S(2)}) copy-start(f32[256,256]{1,0:T(8,128)} %copy-done.21) | copy-start | bytes 786436
  584.9 8.1 copy-start.17
  604.5 7.5 copy-start.47
  657.3 5.1 copy-start.60
  657.3 5.2 copy-start.61
  658.4 143.3 %all-to-all-start.3 = ((f32[32,32,256]{2,1,0:T(8,128)}), f32[32,32,256]{2,1,0:T(8,128)}, u32[]{:S(2)}, u32[]{:S(2)}) async-start(f32[32,32,256]{2,1,0:T(8,128)} %bitcast.94), calls=%async_computation.3 | async-start | bytes 2097152 | tf_op jit(solution)/shard_map/all_to_all | solution.py:75
  662.1 134.5 %all-reduce.12.cloned.1.call-start = ((), (), s32[]{:S(2)}) async-start(), calls=%async_computation.7 | async-start | bytes 524288 | tf_op jit(solution)/shard_map/psum | solution.py:214
  664.8 134.3 %copy-start.75 = (f32[256]{0:T(256)S(1)}, f32[256]{0:T(256)}, u32[]{:S(2)}) copy-start(f32[256]{0:T(256)} %copy-done.74) | copy-start | bytes 3076
  665.9 133.3 %copy-start.55 = (f32[4096]{0:T(1024)S(1)}, f32[4096]{0:T(1024)}, u32[]{:S(2)}) copy-start(f32[4096]{0:T(1024)} %convert_element_type.40) | copy-start | bytes 49156
  801.7 6.8 copy-start.44
  809.4 5.1 copy-start.15
  816.1 7.5 copy-start.48
  823.6 45.3 %copy-start.56 = (s32[4096,1]{0,1:T(1,128)S(1)}, s32[4096,1]{0,1:T(1,128)}, u32[]{:S(2)}) copy-start(s32[4096,1]{0,1:T(1,128)} %compare_select_fusion.1) | copy-start | bytes 49156
  892.7 4.9 copy-start.67
  892.7 4.9 copy-start.77
  893.8 7.8 copy-start.1
  893.8 28.8 %all-to-all-start.4 = ((f32[32,32,256]{2,1,0:T(8,128)}), f32[32,32,256]{2,1,0:T(8,128)}, u32[]{:S(2)}, u32[]{:S(2)}) async-start(f32[32,32,256]{2,1,0:T(8,128)} %bitcast.95), calls=%async_computation.4 | async-start | bytes 2097152 | tf_op jit(solution)/shard_map/all_to_all | solution.py:75
  897.6 172.9 %all-reduce.14.cloned.1.call-start = ((), (), s32[]{:S(2)}) async-start(), calls=%async_computation.8 | async-start | bytes 4243456 | tf_op jit(solution)/shard_map/psum | solution.py:220
  897.7 6.6 copy-start.20
  922.6 8.3 copy-start.24
  938.6 131.8 %copy-start.23 = (f32[256,256]{1,0:T(8,128)S(1)}, f32[256,256]{1,0:T(8,128)}, u32[]{:S(2)}) copy-start(f32[256,256]{1,0:T(8,128)} %copy-done.21) | copy-start | bytes 786436
  938.6 131.8 %copy-start.27 = (f32[256,256]{1,0:T(8,128)S(1)}, f32[256,256]{1,0:T(8,128)}, u32[]{:S(2)}) copy-start(f32[256,256]{1,0:T(8,128)} %copy-done.26) | copy-start | bytes 786436
  938.6 131.8 %copy-start.29 = (f32[256,256]{1,0:T(8,128)S(1)}, f32[256,256]{1,0:T(8,128)}, u32[]{:S(2)}) copy-start(f32[256,256]{1,0:T(8,128)} %copy-done.28) | copy-start | bytes 786436
  940.1 135.4 %copy-start.31 = (f32[256,512]{1,0:T(8,128)S(1)}, f32[256,512]{1,0:T(8,128)}, u32[]{:S(2)}) copy-start(f32[256,512]{1,0:T(8,128)} %copy-done.30) | copy-start | bytes 1572868
  940.1 136.7 %copy-start.10 = (f32[256,602]{0,1:T(8,128)S(1)}, f32[256,602]{0,1:T(8,128)}, u32[]{:S(2)}) copy-start(f32[256,602]{0,1:T(8,128)} %param.25) | copy-start | bytes 1849348
  940.1 136.7 %copy-start.12 = (f32[256,602]{0,1:T(8,128)S(1)}, f32[256,602]{0,1:T(8,128)}, u32[]{:S(2)}) copy-start(f32[256,602]{0,1:T(8,128)} %copy-done.11) | copy-start | bytes 1849348
  1070.4 6.3 copy-start.34
  1076.8 5.1 copy-start.73
  1076.8 5.1 copy-start.79
  1076.8 5.1 copy-start.80
  1076.8 5.7 copy-start.46
  (45 other events, 101.8 us)
Sparse Core Ops, SparseCore 0:
  197.1 129.1 all-reduce.7
  416.8 126.1 all-reduce.9
  670.0 126.6 all-reduce.11
  935.3 135.0 all-reduce.13
where the time goes:
time: 1110 us; the launch traced here: 1100 us
  waiting for transfers between devices  506 us (46%)
  other arithmetic  210 us (19%)
  local copies, waits for them, and re-layouts  198 us (18%)
  blocking collectives  82.1 us (7%)
  matrix products  58.1 us (5%)
  starting transfers between devices  24.7 us (2%)
  between operations  19.3 us (2%)
    psum x1, waiting for transfers between devices, local(): hub_total = lax.psum(table_grad[node_count + halo_count:], ('dom', 'sub'))  131 us
    psum x1, waiting for transfers between devices, local(): hub_sum = lax.psum(hub_partial, ('dom', 'sub'))  126 us
    gather x9, local copies, waits for them, and re-layouts, one_block(): lookup[block_index]  125 us
    scatter-add x2, other arithmetic, local(): table_grad.at[high_lists.reshape(-1)]  90.6 us
    psum x1, waiting for transfers between devices, local(): lax.psum((weight_grads[0], weight_grads[1], weight_grads[2], jnp.concaten...  89 us
    psum x1, waiting for transfers between devices, local(): lax.psum((hub_partial, jnp.sum(hub_weights, axis=1), jnp.sum(train_weight...  85.6 us
    all_to_all x3, waiting for transfers between devices, send_forward(): lax.all_to_all(blocks, ('dom', 'sub'), split_axis=0, concat_axis=0, tiled...  56.6 us
    psum x1, blocking collectives, local(): lax.psum((weight_grads[0], weight_grads[1], weight_grads[2], jnp.concaten...  41.3 us
  transfers between devices with their start and end apart: 9, of which 6 were waited for; matrix products, arithmetic and copies ran while one was open for 8% of the time, Pallas kernels for 0%

commit v1 on v0

v1 whole, which is shorter than its diff:
```python
import functools

import jax
import jax.numpy as jnp
from jax import lax
from jax.experimental import pallas as pl
from jax.experimental.pallas import tpu as pltpu
from jax.sharding import PartitionSpec as P

MESH = pl.DeviceIdType.MESH
F32 = jnp.float32
BF16 = jnp.bfloat16

STEP = 5
KEEP = 0.95
SMOOTH = 0.1
CLIP = 0.02
RATE = 0.03
DECAY = 0.01
EPSILON = 1e-08
CORRECT = 1.0 - 0.5**STEP
GELU_A = 0.7978845608
GELU_B = 0.044715
LANES = 128


def up(value, unit):
    return -(-value // unit) * unit


def split(values):
    high = values.astype(BF16)
    return high, (values - high.astype(F32)).astype(BF16)


def dot(left, right):
    return jnp.dot(left, right, preferred_element_type=F32)


def dot_nt(left, right):
    return lax.dot_general(left, right, (((1,), (1,)), ((), ())), preferred_element_type=F32)


def dot_tn(left, right):
    return lax.dot_general(left, right, (((0,), (0,)), ((), ())), preferred_element_type=F32)


def three(product, left, right):
    return (
        product(left[0], right[1]) + product(left[1], right[0])
    ) + product(left[0], right[0])


def gelu(v):
    return 0.5 * v * (1.0 + jnp.tanh(GELU_A * (v + GELU_B * (v * v * v))))


def gelu_slope(v):
    t = jnp.tanh(GELU_A * (v + GELU_B * (v * v * v)))
    return 0.5 * (1.0 + t) + (0.5 * GELU_A) * v * (1.0 - t * t) * (1.0 + (3.0 * GELU_B) * (v * v))


def tiles(total, step, body):
    @pl.loop(0, total // step)
    def _(index):
        body(pl.multiple_of(index * step, step))


class Sizes:
    def __init__(self, mesh, features, low_lists, high_lists, hub_lists, send_rows, weight_one, weight_three):
        self.dom, self.sub = mesh.shape["dom"], mesh.shape["sub"]
        self.devices = self.dom * self.sub
        self.nodes, self.fin = features.shape
        self.low = low_lists.shape[0]
        self.high = high_lists.shape[0]
        self.hubs = hub_lists.shape[1]
        self.blk = send_rows.shape[2]
        self.halo = self.devices * self.blk
        self.hid = weight_one.shape[1]
        self.cls = weight_three.shape[1]
        self.rows = self.nodes + self.hubs
        self.table = self.nodes + self.halo + self.hubs
        self.fpad = up(self.fin, LANES)
        self.frows = up(self.fin, 8)
        self.shift = self.fin % 8
        self.brows = up(self.fin + self.shift, 8)
        self.part = self.hubs // self.dom
        self.packed = self.blk % 16 == 0
        self.cblk = self.blk // 2 if self.packed else self.blk
        unit = 8 * self.devices
        self.off_two = 2 * self.frows
        self.off_three = self.off_two + 2 * (2 * self.hid)
        self.off_bias = self.off_three + self.hid
        self.rows_early = up(self.off_bias + 8, unit)
        self.rows_late = up(2 * self.brows, unit)


def train_kernel(
    z,
    feat, hubf, lowl, lowm, highl, highm, hubl, hubm, send, lab, tmask, stale_hbm, w1, w2, w3, bias,
    early_hbm, late_hbm, fresh_hbm, misc,
    ab, abt, sel, selt, colb, keys, xh, xl, xth, xtl, w1h, w1l, w2h, w2l, w3h, w3l,
    tb, tc, inv, q, h1h, h1l, m1h, m1l, h2h, h2l, dg0, dg1, dph, dpl, dmh, dml, eb, gown, ghub, stale, newst,
    zst, pself, labc, trainw, bulkh,
    send_a, recv_a, send_b, recv_b, send_c, recv_c, send_d, recv_d, send_e, recv_e, send_f, recv_f, send_g, recv_g,
    hs0, ha0, hb0, hg0, hs1, ha1, hb1, hg1, hs2, ha2, hb2, hg2, hs3, ha3, hb3, hg3, hs4, ha4, hb4, hg4,
    es, ea, ep, ebuf, er, ls, la, lp, lbuf, lr,
    xs, xr, hsem_s, hsem_r, gsem_s, gsem_r, lsem,
):
    d = lax.axis_index("dom")
    s = lax.axis_index("sub")
    me = d * z.sub + s
    nd, halo, hubs, hid = z.nodes, z.halo, z.hubs, z.hid
    halo0, hub0 = nd, nd + halo
    i32 = jnp.int32

    barrier = pltpu.get_barrier_semaphore()

    @pl.loop(1, z.devices)
    def _(k):
        pl.semaphore_signal(
            barrier,
            inc=1,
            device_id=(lax.rem(d + k // z.sub, z.dom), lax.rem(s + k % z.sub, z.sub)),
            device_id_type=MESH,
        )

    stale_copy = pltpu.make_async_copy(stale_hbm, stale, lsem.at[0])
    stale_copy.start()

    def remote(src, dst, ssem, rsem, pd, ps):
        return pltpu.make_async_remote_copy(
            src_ref=src, dst_ref=dst, send_sem=ssem, recv_sem=rsem, device_id=(pd, ps), device_id_type=MESH
        )

    def exchange_start(src, dst, i):
        @pl.loop(1, z.devices)
        def _(k):
            pd = lax.rem(d + k // z.sub, z.dom)
            ps = lax.rem(s + k % z.sub, z.sub)
            remote(src.at[pd * z.sub + ps], dst.at[me], xs.at[i], xr.at[i], pd, ps).start()

        dst[me] = src[me]

    def exchange_wait(src, dst, i):
        some = pl.ds(0, z.devices - 1)
        copy = remote(src.at[some], dst.at[some], xs.at[i], xr.at[i], lax.rem(d + 1, z.dom), s)
        copy.wait_recv()
        copy.wait_send()

    def hub_scatter(src, ra, i):
        @pl.loop(1, z.dom)
        def _(k):
            pd = lax.rem(d + k, z.dom)
            remote(src.at[pd], ra.at[d], hsem_s.at[i, 0], hsem_r.at[i, 0], pd, s).start()

        ra[d] = src[d]

    def hub_swap(src, ra, rb, i):
        some = pl.ds(0, z.dom - 1)
        copy = remote(src.at[some], ra.at[some], hsem_s.at[i, 0], hsem_r.at[i, 0], lax.rem(d + 1, z.dom), s)
        copy.wait_recv()
        total = ra[0]
        for k in range(1, z.dom):
            total = total + ra[k]
        rb[s] = total

        @pl.loop(1, z.sub)
        def _(k):
            ps = lax.rem(s + k, z.sub)
            remote(rb.at[s], rb.at[s], hsem_s.at[i, 1], hsem_r.at[i, 1], d, ps).start()

        copy.wait_send()

    def hub_gather(rb, rg, i):
        some = pl.ds(0, z.sub - 1)
        copy = remote(rb.at[some], rb.at[some], hsem_s.at[i, 1], hsem_r.at[i, 1], d, lax.rem(s + 1, z.sub))
        copy.wait_recv()
        total = rb[0]
        for k in range(1, z.sub):
            total = total + rb[k]
        rg[d] = total

        @pl.loop(1, z.dom)
        def _(k):
            pd = lax.rem(d + k, z.dom)
            remote(rg.at[d], rg.at[d], hsem_s.at[i, 2], hsem_r.at[i, 2], pd, s).start()

        copy.wait_send()

    def hub_end(rg, i):
        some = pl.ds(0, z.dom - 1)
        copy = remote(rg.at[some], rg.at[some], hsem_s.at[i, 2], hsem_r.at[i, 2], lax.rem(d + 1, z.dom), s)
        copy.wait_recv()
        copy.wait_send()

    def hub_value(rg):
        return rg[...].reshape(hubs, rg.shape[-1])

    def grad_scatter(src, ra, i):
        big = src.shape[0] // z.dom

        @pl.loop(1, z.dom)
        def _(k):
            pd = lax.rem(d + k, z.dom)
            remote(
                src.at[pl.ds(pl.multiple_of(pd * big, 8), big)], ra.at[d], gsem_s.at[i, 0], gsem_r.at[i, 0], pd, s
            ).start()

    def grad_swap(src, ra, rp, rb, i):
        big = src.shape[0] // z.dom
        small = big // z.sub
        some = pl.ds(0, z.dom - 1)
        ra[d] = src[pl.ds(pl.multiple_of(d * big, 8), big), :]
        copy = remote(ra.at[some], ra.at[some], gsem_s.at[i, 0], gsem_r.at[i, 0], lax.rem(d + 1, z.dom), s)
        copy.wait_recv()
        total = ra[0]
        for k in range(1, z.dom):
            total = total + ra[k]
        rp[...] = total

        @pl.loop(1, z.sub)
        def _(k):
            ps = lax.rem(s + k, z.sub)
            remote(
                rp.at[pl.ds(pl.multiple_of(ps * small, 8), small)], rb.at[s], gsem_s.at[i, 1], gsem_r.at[i, 1], d, ps
            ).start()

        copy.wait_send()

    def grad_sub_gather(src, rp, rb, res, i):
        big = src.shape[0] // z.dom
        small = big // z.sub
        some = pl.ds(0, z.sub - 1)
        rb[s] = rp[pl.ds(pl.multiple_of(s * small, 8), small), :]
        copy = remote(rb.at[some], rb.at[some], gsem_s.at[i, 1], gsem_r.at[i, 1], d, lax.rem(s + 1, z.sub))
        copy.wait_recv()
        total = rb[0]
        for k in range(1, z.sub):
            total = total + rb[k]
        mine = pl.ds(pl.multiple_of(me * small, 8), small)
        res[mine, :] = total

        @pl.loop(1, z.sub)
        def _(k):
            ps = lax.rem(s + k, z.sub)
            remote(res.at[mine], res.at[mine], gsem_s.at[i, 2], gsem_r.at[i, 2], d, ps).start()

        copy.wait_send()

    def grad_dom_gather(res, i):
        big = res.shape[0] // z.dom
        small = big // z.sub
        some = pl.ds(0, big - small)
        copy = remote(res.at[some], res.at[some], gsem_s.at[i, 2], gsem_r.at[i, 2], d, lax.rem(s + 1, z.sub))
        copy.wait_recv()
        group = pl.ds(pl.multiple_of(d * big, 8), big)

        @pl.loop(1, z.dom)
        def _(k):
            pd = lax.rem(d + k, z.dom)
            remote(res.at[group], res.at[group], gsem_s.at[i, 3], gsem_r.at[i, 3], pd, s).start()

        copy.wait_send()

    def grad_end(res, i):
        big = res.shape[0] // z.dom
        some = pl.ds(0, res.shape[0] - big)
        copy = remote(res.at[some], res.at[some], gsem_s.at[i, 3], gsem_r.at[i, 3], lax.rem(d + 1, z.dom), s)
        copy.wait_recv()
        copy.wait_send()

    def put_split(ref, rows, values):
        width = values.shape[1]
        high, rest = split(values)
        ref[rows, 0:width] = high
        ref[rows, width : 2 * width] = rest

    def both(left, right):
        width = right.shape[1] // 2
        return dot(left, right[:, width:]) + dot(left, right[:, :width])

    per_tile = 256 // z.blk

    xh[:, 512 : z.fpad] = jnp.zeros((z.rows, z.fpad - 512), BF16)
    xl[:, 512 : z.fpad] = jnp.zeros((z.rows, z.fpad - 512), BF16)
    w1h[512 : z.fpad, :] = jnp.zeros((z.fpad - 512, 2 * hid), BF16)
    w1l[512 : z.fpad, :] = jnp.zeros((z.fpad - 512, 2 * hid), BF16)
    high, rest = split(feat[...])
    xh[0:nd, 0 : z.fin] = high
    xl[0:nd, 0 : z.fin] = rest
    high, rest = split(w1[z.fin : 2 * z.fin, :])
    w1h[0 : z.fin, hid : 2 * hid] = high
    w1l[0 : z.fin, hid : 2 * hid] = rest

    def project(rows, columns):
        return three(dot, (xh[rows, :], xl[rows, :]), (w1h[:, columns], w1l[:, columns]))

    tiles(nd, 256, lambda r: put_split(tb, pl.ds(r, 256), project(pl.ds(r, 256), slice(hid, 2 * hid))))

    eye = lax.broadcasted_iota(i32, (z.blk, z.blk), 0) == lax.broadcasted_iota(i32, (z.blk, z.blk), 1)

    @pl.loop(0, z.devices)
    def _(p):
        line = jnp.broadcast_to(send[pl.ds(p, 1), :], (z.blk, z.blk))
        colb[pl.ds(pl.multiple_of(p * z.blk, z.blk), z.blk), :] = jnp.sum(
            jnp.where(eye, line, 0), axis=1, keepdims=True
        )

    def pick_tile(r):
        rows = pl.ds(r, 256)
        chosen = jnp.where(colb[rows, :] == lax.broadcasted_iota(i32, (256, nd), 1), 1.0, 0.0).astype(BF16)
        sel[rows, :] = chosen
        values = both(chosen, tb[0:nd, :])
        send_a[pl.ds(r // z.blk, per_tile)] = values.reshape(per_tile, z.blk, hid)

    tiles(halo, 256, pick_tile)
    pl.semaphore_wait(barrier, z.devices - 1)
    exchange_start(send_a, recv_a, 0)

    weights = lowm[...].astype(F32)
    inv[0 : z.low, :] = 1.0 / jnp.maximum(jnp.sum(weights, axis=1, keepdims=True), 1.0)
    weights = highm[...].astype(F32)
    inv[z.low : nd, :] = 1.0 / jnp.maximum(jnp.sum(weights, axis=1, keepdims=True), 1.0)
    diag = lax.broadcasted_iota(i32, (LANES, LANES), 0) == lax.broadcasted_iota(i32, (LANES, LANES), 1)
    for block in range(nd // LANES):
        rows = slice(block * LANES, (block + 1) * LANES)
        line = jnp.broadcast_to(lab[block : block + 1, :], (LANES, LANES))
        labc[rows, :] = jnp.sum(jnp.where(diag, line, 0), axis=1, keepdims=True)
        line = jnp.broadcast_to(tmask[block : block + 1, :].astype(F32), (LANES, LANES))
        trainw[rows, :] = jnp.sum(jnp.where(diag, line, 0.0), axis=1, keepdims=True)
    train_local = jnp.sum(jnp.sum(tmask[...].astype(F32), axis=1, keepdims=True), axis=0, keepdims=True)
    hub_local = jnp.sum(hubm[...].astype(F32), axis=1, keepdims=True)
    lane = lax.broadcasted_iota(i32, (hubs, LANES), 1)
    hs0[...] = jnp.where(lane == 0, hub_local, jnp.where(lane == 1, train_local, 0.0)).reshape(hs0.shape)
    hub_scatter(hs0, ha0, 0)

    keys[0 : z.low, 0 : lowl.shape[1]] = jnp.where(lowm[...] > 0, lowl[...], -1)
    keys[z.low : nd, 0 : highl.shape[1]] = jnp.where(highm[...] > 0, highl[...], -1)
    keys[nd : z.rows, 0 : hubl.shape[1]] = jnp.where(hubm[...] > 0, hubl[...], -1)

    def build(first, count, slots):
        width = z.table // 2

        def group(r):
            rows = pl.ds(first + r, 16)
            key = keys[rows, 0:LANES]
            for half in range(2):
                place = lax.broadcasted_iota(i32, (16, width), 1) + half * width
                total = jnp.zeros((16, width), F32)
                for k in range(slots):
                    total = total + jnp.where(key[:, k : k + 1] == place, 1.0, 0.0)
                ab[rows, half * width : (half + 1) * width] = total.astype(BF16)

        tiles(count, 16, group)

    build(0, z.low, lowl.shape[1])
    hub_swap(hs0, ha0, hb0, 0)
    build(nd, hubs, hubl.shape[1])
    hub_gather(hb0, hg0, 0)
    build(z.low, z.high, highl.shape[1])

    high, rest = split(hubf[...])
    xh[nd : z.rows, 0 : z.fin] = high
    xl[nd : z.rows, 0 : z.fin] = rest
    high, rest = split(w1[0 : z.fin, :])
    w1h[0 : z.fin, 0:hid] = high
    w1l[0 : z.fin, 0:hid] = rest
    put_split(tb, slice(hub0, z.table), project(slice(nd, z.rows), slice(hid, 2 * hid)))

    def own_tile(r):
        rows = pl.ds(r, 256)
        q[rows, :] = project(rows, slice(0, hid)) + bias[0:1, :]

    tiles(z.rows, 256, own_tile)
    high, rest = split(w2[...])
    w2h[...] = high
    w2l[...] = rest
    w3h[:, :] = jnp.zeros(w3h.shape, BF16)
    w3l[:, :] = jnp.zeros(w3l.shape, BF16)
    high, rest = split(w3[...])
    w3h[:, 0 : z.cls] = high
    w3l[:, 0 : z.cls] = rest
    hub_end(hg0, 0)
    sums = hub_value(hg0)
    inv[nd : z.rows, :] = 1.0 / sums[:, 0:1]
    misc[...] = sums[0:8, :]
    train_total = sums[0:1, 1:2]

    exchange_wait(send_a, recv_a, 0)
    put_split(tb, slice(halo0, hub0), recv_a[...].reshape(halo, hid))
    hs1[...] = both(ab[nd : z.rows, :], tb[...]).reshape(hs1.shape)
    hub_scatter(hs1, ha1, 1)

    def layer_one(r):
        rows = pl.ds(r, 256)
        pre = q[rows, :] + both(ab[rows, :], tb[...]) * inv[rows, :]
        q[rows, :] = pre
        high, rest = split(gelu(pre))
        h1h[rows, :] = high
        h1l[rows, :] = rest

    tiles(nd, 256, layer_one)
    tb[0:nd, 0:hid] = h1h[0:nd, :]
    tb[0:nd, hid : 2 * hid] = h1l[0:nd, :]

    def pick(target):
        def body(r):
            values = both(sel[pl.ds(r, 256), :], tb[0:nd, :])
            target[pl.ds(r // z.blk, per_tile)] = values.reshape(per_tile, z.blk, hid)

        tiles(halo, 256, body)

    pick(send_b)
    exchange_start(send_b, recv_b, 1)

    def turn(source, target, r_count, c_count, step=128):
        def body(r):
            for c in range(0, c_count, step):
                target[c : c + step, pl.ds(r, step)] = source[pl.ds(r, step), c : c + step].T

        tiles(r_count, step, body)

    hub_swap(hs1, ha1, hb1, 1)
    turn(ab, abt, z.rows, z.table)
    hub_gather(hb1, hg1, 1)
    turn(sel, selt, halo, nd)
    turn(xh, xth, z.rows, z.fpad)
    turn(xl, xtl, z.rows, z.fpad)
    stale_copy.wait()
    zst[...] = three(dot, split(KEEP * stale[1]), (w3h[hid : 2 * hid, :], w3l[hid : 2 * hid, :]))
    dg0[0:nd, :] = gelu_slope(q[0:nd, :])
    hub_end(hg1, 1)
    pre = q[nd : z.rows, :] + hub_value(hg1) * inv[nd : z.rows, :]
    dg0[nd : z.rows, :] = gelu_slope(pre)
    high, rest = split(gelu(pre))
    h1h[nd : z.rows, :] = high
    h1l[nd : z.rows, :] = rest
    tb[hub0 : z.table, 0:hid] = high
    tb[hub0 : z.table, hid : 2 * hid] = rest

    def own_two(r):
        rows = pl.ds(r, 256)
        q[rows, :] = three(dot, (h1h[rows, :], h1l[rows, :]), (w2h[0:hid, :], w2l[0:hid, :])) + bias[1:2, :]

    tiles(z.rows, 256, own_two)

    exchange_wait(send_b, recv_b, 1)

    def renew(slot, recv):
        newst[slot] = KEEP * stale[slot] + (1.0 - KEEP) * recv[...].reshape(halo, hid)

    renew(0, recv_b)
    put_split(tb, slice(halo0, hub0), newst[0])
    hs2[...] = both(ab[nd : z.rows, :], tb[...]).reshape(hs2.shape)
    hub_scatter(hs2, ha2, 2)

    def layer_two(r):
        rows = pl.ds(r, 256)
        mean = split(both(ab[rows, :], tb[...]) * inv[rows, :])
        m1h[rows, :] = mean[0]
        m1l[rows, :] = mean[1]
        pre = q[rows, :] + three(dot, mean, (w2h[hid : 2 * hid, :], w2l[hid : 2 * hid, :]))
        q[rows, :] = pre
        high, rest = split(gelu(pre))
        h2h[rows, :] = high
        h2l[rows, :] = rest
        put_split(tc, rows, three(dot, (high, rest), (w3h[hid : 2 * hid, :], w3l[hid : 2 * hid, :])))

    tiles(nd, 256, layer_two)
    class_lane = lax.broadcasted_iota(i32, (1, 1, LANES), 2) < LANES // 2

    def pack(values):
        groups = values.shape[0] // z.blk
        blocks = values.reshape(groups, z.blk, LANES)
        if z.packed:
            return blocks[:, : z.cblk] + pltpu.roll(blocks[:, z.cblk :], LANES // 2, 2)
        return blocks

    def unpack(blocks):
        if z.packed:
            first = jnp.where(class_lane, blocks, 0.0)
            second = jnp.where(class_lane, pltpu.roll(blocks, LANES // 2, 2), 0.0)
            blocks = jnp.concatenate([first, second], axis=1)
        return blocks.reshape(halo, LANES)

    def pick_class(r):
        values = both(sel[pl.ds(r, 256), :], tc[0:nd, :])
        send_c[pl.ds(r // z.blk, per_tile)] = pack(values)

    tiles(halo, 256, pick_class)
    exchange_start(send_c, recv_c, 2)
    hub_swap(hs2, ha2, hb2, 2)

    def own_three(r):
        rows = pl.ds(r, 256)
        pself[rows, :] = three(dot, (h2h[rows, :], h2l[rows, :]), (w3h[0:hid, :], w3l[0:hid, :])) + bias[2:3, 0:LANES]

    tiles(nd, 256, own_three)
    hub_gather(hb2, hg2, 2)
    dg1[0:nd, :] = gelu_slope(q[0:nd, :])
    hub_end(hg2, 2)
    mean = split(hub_value(hg2) * inv[nd : z.rows, :])
    m1h[nd : z.rows, :] = mean[0]
    m1l[nd : z.rows, :] = mean[1]
    pre = q[nd : z.rows, :] + three(dot, mean, (w2h[hid : 2 * hid, :], w2l[hid : 2 * hid, :]))
    high, rest = split(gelu(pre))
    h2h[nd : z.rows, :] = high
    h2l[nd : z.rows, :] = rest
    put_split(tc, slice(hub0, z.table), three(dot, (high, rest), (w3h[hid : 2 * hid, :], w3l[hid : 2 * hid, :])))
    q[nd : z.rows, :] = pre

    exchange_wait(send_c, recv_c, 2)
    put_split(tc, slice(halo0, hub0), zst[...] + (1.0 - KEEP) * unpack(recv_c[...]))
    used = lax.broadcasted_iota(i32, (256, LANES), 1)
    es[...] = jnp.zeros(es.shape, F32)
    ls[...] = jnp.zeros(ls.shape, F32)

    def head(r):
        rows = pl.ds(r, 256)
        logits = pself[rows, :] + both(ab[rows, :], tc[...]) * inv[rows, :]
        valid = used < z.cls
        top = jnp.max(jnp.where(valid, logits, -1e30), axis=1, keepdims=True)
        shifted = logits - top
        powers = jnp.where(valid, jnp.exp(jnp.where(valid, shifted, 0.0)), 0.0)
        total = jnp.sum(powers, axis=1, keepdims=True)
        log_probs = jnp.where(valid, shifted - jnp.log(total), 0.0)
        target = jnp.where(used == labc[rows, :], 1.0 - SMOOTH, 0.0) + SMOOTH / z.cls
        weight = trainw[rows, :]
        losses = jnp.sum(jnp.where(valid, -target * log_probs, 0.0), axis=1, keepdims=True) * weight
        grad = jnp.where(valid, powers / total - target, 0.0) * weight / train_total
        es[z.off_bias + 4 : z.off_bias + 5, :] = es[z.off_bias + 4 : z.off_bias + 5, :] + jnp.sum(
            grad, axis=0, keepdims=True
        )
        es[z.off_bias + 5 : z.off_bias + 6, :] = es[z.off_bias + 5 : z.off_bias + 6, :] + jnp.sum(
            losses, axis=0, keepdims=True
        )
        high, rest = split(grad)
        dph[rows, 0:LANES] = high
        dpl[rows, 0:LANES] = rest
        high, rest = split(grad * inv[rows, :])
        eb[rows, 0:LANES] = high
        eb[rows, LANES : 2 * LANES] = rest

    tiles(nd, 256, head)

    hub_class = both(abt[hub0 : z.table, 0:nd], eb[0:nd, 0 : 2 * LANES])
    hs3[...] = hub_class.reshape(hs3.shape)
    hub_scatter(hs3, ha3, 3)

    def back_class(r):
        values = both(abt[pl.ds(halo0 + r, 256), 0:nd], eb[0:nd, 0 : 2 * LANES])
        put_split(tc, pl.ds(halo0 + r, 256), values)
        send_d[pl.ds(r // z.blk, per_tile)] = pack((1.0 - KEEP) * values)

    tiles(halo, 256, back_class)
    exchange_start(send_d, recv_d, 3)
    hub_swap(hs3, ha3, hb3, 3)
    gown[0:nd, 0:LANES] = both(abt[0:nd, 0:nd], eb[0:nd, 0 : 2 * LANES])
    hub_gather(hb3, hg3, 3)

    lower = three(dot_tn, split(KEEP * stale[1]), (tc[halo0:hub0, 0:LANES], tc[halo0:hub0, LANES : 2 * LANES]))
    lower = lower + three(dot_tn, (h2h[nd : z.rows, :], h2l[nd : z.rows, :]), split(hub_class))
    ghub[:, 0:LANES] = lower
    ghub[:, LANES : 2 * LANES] = three(dot_tn, (h2h[0:nd, :], h2l[0:nd, :]), (dph[0:nd, 0:LANES], dpl[0:nd, 0:LANES]))
    dg1[nd : z.rows, :] = gelu_slope(q[nd : z.rows, :])

    hub_end(hg3, 3)
    node = three(dot_nt, split(hub_value(hg3)), (w3h[hid : 2 * hid, :], w3l[hid : 2 * hid, :])) * dg1[nd : z.rows, :]
    high, rest = split(node)
    dph[nd : z.rows, :] = high
    dpl[nd : z.rows, :] = rest

    def owned(values):
        row = lax.broadcasted_iota(i32, (hubs, 1), 0)
        share = hubs // z.devices
        mine = jnp.where(row >= me * share, 1.0, 0.0) * jnp.where(row < (me + 1) * share, 1.0, 0.0)
        return values * mine

    def hub_own(values):
        high, rest = split(owned(values))
        dmh[nd : z.rows, :] = high
        dml[nd : z.rows, :] = rest

    def column_sums(lanes):
        return jnp.sum(dmh[:, lanes].astype(F32) + dml[:, lanes].astype(F32), axis=0, keepdims=True)

    hub_own(node)
    exchange_wait(send_d, recv_d, 3)
    put_split(tc, slice(halo0, hub0), unpack(recv_d[...]))
    own_class = gown[0:nd, 0:LANES] + both(selt[...], tc[halo0:hub0, :])
    gown[0:nd, 0:LANES] = own_class
    own_class = split(own_class)
    node = (
        three(dot_nt, own_class, (w3h[hid : 2 * hid, :], w3l[hid : 2 * hid, :]))
        + three(dot_nt, (dph[0:nd, 0:LANES], dpl[0:nd, 0:LANES]), (w3h[0:hid, :], w3l[0:hid, :]))
    ) * dg1[0:nd, :]
    high, rest = split(node)
    dph[0:nd, :] = high
    dpl[0:nd, :] = rest
    dmh[0:nd, :] = high
    dml[0:nd, :] = rest

    def spread(r):
        rows = pl.ds(r, 256)
        values = three(dot_nt, (dph[rows, :], dpl[rows, :]), (w2h[hid : 2 * hid, :], w2l[hid : 2 * hid, :]))
        put_split(eb, rows, values * inv[rows, :])

    tiles(z.rows, 256, spread)
    hs4[...] = both(abt[hub0 : z.table, :], eb[...]).reshape(hs4.shape)
    hub_scatter(hs4, ha4, 4)

    def send_halo(target, factor):
        def body(r):
            values = both(abt[pl.ds(halo0 + r, 256), :], eb[...]) * factor
            target[pl.ds(r // z.blk, per_tile)] = values.reshape(per_tile, z.blk, hid)

        tiles(halo, 256, body)

    send_halo(send_e, 1.0 - KEEP)
    exchange_start(send_e, recv_e, 4)
    hub_swap(hs4, ha4, hb4, 4)

    lower = ghub[:, 0:LANES] + three(dot_tn, (h2h[0:nd, :], h2l[0:nd, :]), split(gown[0:nd, 0:LANES]))
    es[z.off_three : z.off_three + hid, :] = ghub[:, LANES : 2 * LANES] + pltpu.roll(lower, LANES // 2, 1)

    def own_back(r):
        rows = pl.ds(r, 256)
        q[rows, :] = three(dot_nt, (dph[rows, :], dpl[rows, :]), (w2h[0:hid, :], w2l[0:hid, :]))

    tiles(z.rows, 256, own_back)

    def own_table(r):
        rows = pl.ds(r, 256)
        q[rows, :] = q[rows, :] + both(abt[rows, :], eb[...])

    tiles(nd, 256, own_table)
    hub_gather(hb4, hg4, 4)
    for half in range(2):
        lanes = slice(half * LANES, (half + 1) * LANES)
        start = z.off_two + half * 2 * hid
        es[start : start + hid, :] = three(dot_tn, (h1h[...], h1l[...]), (dmh[:, lanes], dml[:, lanes]))
        es[start + hid : start + 2 * hid, :] = three(dot_tn, (m1h[...], m1l[...]), (dmh[:, lanes], dml[:, lanes]))
        es[z.off_bias + 2 + half : z.off_bias + 3 + half, :] = column_sums(lanes)

    tb[0:nd, 0:hid] = h2h[0:nd, :]
    tb[0:nd, hid : 2 * hid] = h2l[0:nd, :]
    pick(send_g)
    hub_end(hg4, 4)
    node = (hub_value(hg4) + q[nd : z.rows, :]) * dg0[nd : z.rows, :]
    high, rest = split(node)
    dph[nd : z.rows, :] = high
    dpl[nd : z.rows, :] = rest
    hub_own(node)
    put_split(eb, slice(nd, z.rows), node * inv[nd : z.rows, :])

    exchange_wait(send_e, recv_e, 4)
    put_split(tb, slice(halo0, hub0), recv_e[...].reshape(halo, hid))
    node = (q[0:nd, :] + both(selt[...], tb[halo0:hub0, :])) * dg0[0:nd, :]
    high, rest = split(node)
    dmh[0:nd, :] = high
    dml[0:nd, :] = rest
    put_split(eb, slice(0, nd), node * inv[0:nd, :])

    send_halo(send_f, 1.0)
    exchange_start(send_f, recv_f, 5)
    one_upper = three(dot, (xth[...], xtl[...]), (dmh[...], dml[...]))
    for half in range(2):
        lanes = slice(half * LANES, (half + 1) * LANES)
        es[half * z.frows : (half + 1) * z.frows, :] = one_upper[0 : z.frows, lanes]
        es[z.off_bias + half : z.off_bias + 1 + half, :] = column_sums(lanes)
    grad_scatter(es, ea, 0)

    def own_last(r):
        gown[pl.ds(r, 256), :] = both(abt[pl.ds(r, 256), :], eb[...])

    tiles(nd, 256, own_last)
    high, rest = split(both(abt[hub0 : z.table, :], eb[...]))
    dmh[nd : z.rows, :] = high
    dml[nd : z.rows, :] = rest
    grad_swap(es, ea, ep, ebuf, 0)
    grad_sub_gather(es, ep, ebuf, er, 0)
    grad_dom_gather(er, 0)

    exchange_wait(send_f, recv_f, 5)
    exchange_start(send_g, recv_g, 6)
    put_split(tb, slice(halo0, hub0), recv_f[...].reshape(halo, hid))
    high, rest = split(gown[...] + both(selt[...], tb[halo0:hub0, :]))
    dmh[0:nd, :] = high
    dml[0:nd, :] = rest
    one_lower = three(dot, (xth[...], xtl[...]), (dmh[...], dml[...]))
    for half in range(2):
        lanes = slice(half * LANES, (half + 1) * LANES)
        start = half * z.brows + z.shift
        ls[start : start + z.fin, :] = one_lower[0 : z.fin, lanes]
    grad_scatter(ls, la, 1)
    grad_end(er, 0)
    early_copy = pltpu.make_async_copy(er, early_hbm, lsem.at[1])
    early_copy.start()
    grad_swap(ls, la, lp, lbuf, 1)
    grad_sub_gather(ls, lp, lbuf, lr, 1)
    grad_dom_gather(lr, 1)
    exchange_wait(send_g, recv_g, 6)
    renew(1, recv_g)
    fresh_copy = pltpu.make_async_copy(newst, fresh_hbm, lsem.at[2])
    fresh_copy.start()
    grad_end(lr, 1)
    late_copy = pltpu.make_async_copy(lr, late_hbm, lsem.at[3])
    late_copy.start()
    early_copy.wait()
    fresh_copy.wait()
    late_copy.wait()


def train(z, *args):
    b, f, i = BF16, F32, jnp.int32
    vmem = pltpu.VMEM
    n, rows, tab, hid, halo = z.nodes, z.rows, z.table, z.hid, z.halo
    wide = (z.devices, z.blk, hid)
    thin = (z.devices, z.cblk, LANES)

    def hub_buffers(width):
        return [
            vmem((z.dom, z.part, width), f),
            vmem((z.dom, z.part, width), f),
            vmem((z.sub, z.part, width), f),
            vmem((z.dom, z.part, width), f),
        ]

    def grad_buffers(total):
        big = total // z.dom
        return [
            vmem((total, LANES), f),
            vmem((z.dom, big, LANES), f),
            vmem((big, LANES), f),
            vmem((z.sub, big // z.sub, LANES), f),
            vmem((total, LANES), f),
        ]

    scratch = [
        vmem((rows, tab), b), vmem((tab, rows), b), vmem((halo, n), b), vmem((n, halo), b), vmem((halo, 1), i),
        vmem((rows, LANES), i),
        vmem((rows, z.fpad), b), vmem((rows, z.fpad), b), vmem((z.fpad, rows), b), vmem((z.fpad, rows), b),
        vmem((z.fpad, 2 * hid), b), vmem((z.fpad, 2 * hid), b),
        vmem((2 * hid, hid), b), vmem((2 * hid, hid), b), vmem((2 * hid, LANES), b), vmem((2 * hid, LANES), b),
        vmem((tab, 2 * hid), b), vmem((tab, 2 * LANES), b), vmem((rows, 1), f), vmem((rows, hid), f),
        *[vmem((rows, hid), b) for _ in range(6)],
        vmem((rows, hid), f), vmem((rows, hid), f),
        *[vmem((rows, hid), b) for _ in range(4)],
        vmem((rows, 2 * hid), b), vmem((n, hid), f), vmem((z.hubs, hid), f),
        vmem((2, halo, hid), f), vmem((2, halo, hid), f),
        vmem((halo, LANES), f), vmem((n, LANES), f), vmem((n, 1), i), vmem((n, 1), f), vmem((8, LANES), f),
        vmem(wide, f), vmem(wide, f), vmem(wide, f), vmem(wide, f),
        vmem(thin, f), vmem(thin, f), vmem(thin, f), vmem(thin, f),
        vmem(wide, f), vmem(wide, f), vmem(wide, f), vmem(wide, f), vmem(wide, f), vmem(wide, f),
        *hub_buffers(LANES), *hub_buffers(hid), *hub_buffers(hid), *hub_buffers(LANES), *hub_buffers(hid),
        *grad_buffers(z.rows_early), *grad_buffers(z.rows_late),
        pltpu.SemaphoreType.DMA((7,)), pltpu.SemaphoreType.DMA((7,)),
        pltpu.SemaphoreType.DMA((5, 3)), pltpu.SemaphoreType.DMA((5, 3)),
        pltpu.SemaphoreType.DMA((2, 4)), pltpu.SemaphoreType.DMA((2, 4)),
        pltpu.SemaphoreType.DMA((4,)),
    ]
    inside = pl.BlockSpec(memory_space=pltpu.VMEM)
    outside = pl.BlockSpec(memory_space=pl.ANY)
    return pl.pallas_call(
        functools.partial(train_kernel, z),
        out_shape=(
            jax.ShapeDtypeStruct((z.rows_early, LANES), f),
            jax.ShapeDtypeStruct((z.rows_late, LANES), f),
            jax.ShapeDtypeStruct((2, halo, hid), f),
            jax.ShapeDtypeStruct((8, LANES), f),
        ),
        in_specs=[inside] * 11 + [outside] + [inside] * 4,
        out_specs=(outside, outside, outside, inside),
        scratch_shapes=scratch,
        compiler_params=pltpu.CompilerParams(
            collective_id=0, has_side_effects=True, vmem_limit_bytes=62 * 1024 * 1024
        ),
        name="train",
    )(*args)


def update_kernel(z, early, late, w1, w2, w3, bs, m1, m2, m3, mb, v1, v2, v3, vb,
                  o_norm, o1, o2, o3, ob, n1, n2, n3, nb, s1, s2, s3, sb, c1, c2, c3, cb):
    def squares(values):
        return jnp.sum(jnp.sum(values * values, axis=0, keepdims=True), axis=1, keepdims=True)

    whole = early[0 : z.off_bias, :]
    row = early[z.off_bias : z.off_bias + 5, :]
    norm = jnp.sqrt(squares(whole) + squares(row) + squares(late[0 : 2 * z.brows, :]))
    o_norm[...] = norm
    factor = jnp.minimum(1.0, CLIP / (norm + 1e-06))

    def renew(rows, lanes, grad, w, m, v, ow, om, ov):
        clipped = grad * factor
        moment = 0.5 * m[rows, lanes] + 0.5 * clipped
        second = 0.5 * v[rows, lanes] + 0.5 * clipped * clipped
        old = w[rows, lanes]
        om[rows, lanes] = moment
        ov[rows, lanes] = second
        ow[rows, lanes] = old - RATE * (
            (moment / CORRECT) / (jnp.sqrt(second / CORRECT) + EPSILON) + DECAY * old
        )

    low = z.fin - z.shift
    for half in range(2):
        lanes = slice(half * LANES, (half + 1) * LANES)
        e0, l0 = half * z.frows, half * z.brows
        one = (w1, m1, v1, o1, n1, s1)
        renew(slice(0, low), lanes, early[e0 : e0 + low, :], *one)
        if z.shift:
            renew(
                slice(low, low + 8), lanes, early[e0 + low : e0 + low + 8, :] + late[l0 : l0 + 8, :], *one
            )
            renew(slice(low + 8, 2 * z.fin), lanes, late[l0 + 8 : l0 + z.fin + z.shift, :], *one)
        else:
            renew(slice(low, 2 * z.fin), lanes, late[l0 : l0 + z.fin, :], *one)
        start = z.off_two + half * 2 * z.hid
        renew(slice(0, 2 * z.hid), lanes, early[start : start + 2 * z.hid, :], w2, m2, v2, o2, n2, s2)
        both = early[z.off_three : z.off_three + z.hid, :]
        if half:
            both = pltpu.roll(both, LANES // 2, 1)
        renew(
            slice(half * z.hid, (half + 1) * z.hid), slice(0, z.cls), both[:, 0 : z.cls], w3, m3, v3, o3, n3, s3
        )
    flat = jnp.concatenate([early[z.off_bias + k : z.off_bias + k + 1, :] for k in range(5)], axis=1)
    wide = slice(0, bs.shape[1])
    renew(slice(0, 1), wide, flat[:, wide], bs, mb, vb, ob, nb, sb)
    c1[...] = o1[...].astype(BF16)
    c2[...] = o2[...].astype(BF16)
    c3[...] = o3[...].astype(BF16)
    cb[...] = ob[...].astype(BF16)


def update(z, *args):
    weights = args[2:6]
    same = [jax.ShapeDtypeStruct(w.shape, F32) for w in weights]
    copies = [jax.ShapeDtypeStruct(w.shape, BF16) for w in weights]
    inside = pl.BlockSpec(memory_space=pltpu.VMEM)
    shapes = [jax.ShapeDtypeStruct((1, 1), F32), *same, *same, *same, *copies]
    return pl.pallas_call(
        functools.partial(update_kernel, z),
        out_shape=tuple(shapes),
        in_specs=[inside] * len(args),
        out_specs=tuple([inside] * len(shapes)),
        compiler_params=pltpu.CompilerParams(vmem_limit_bytes=62 * 1024 * 1024),
        name="update",
    )(*args)


def solution(mesh):
    def local(
        features, hub_features, low_lists, low_masks, high_lists, high_masks, hub_lists, hub_masks, send_rows,
        labels, train_mask, stale_rows, weight_one, weight_two, weight_three, biases,
        mean_one, mean_two, mean_three, mean_biases, square_one, square_two, square_three, square_biases,
    ):
        z = Sizes(mesh, features, low_lists, high_lists, hub_lists, send_rows, weight_one, weight_three)
        hid, cls = z.hid, z.cls
        rows = jnp.pad(biases, (0, 3 * hid - biases.shape[0])).reshape(3, hid)
        early, late, renewed, misc = train(
            z, features, hub_features, low_lists, low_masks, high_lists, high_masks, hub_lists[0], hub_masks[0],
            send_rows[0], labels.reshape(-1, LANES), train_mask.reshape(-1, LANES), stale_rows,
            weight_one, weight_two, weight_three, rows,
        )
        line = lambda v: v.reshape(1, -1)
        norm, o1, o2, o3, ob, n1, n2, n3, nb, s1, s2, s3, sb, c1, c2, c3, cb = update(
            z, early, late, weight_one, weight_two, weight_three, line(biases),
            mean_one, mean_two, mean_three, line(mean_biases),
            square_one, square_two, square_three, line(square_biases),
        )
        flat = lambda v: v.reshape(-1)
        return (
            norm[0, 0], early[z.off_bias + 5, 0], misc[0, 1],
            o1, o2, o3, flat(ob), n1, n2, n3, flat(nb), s1, s2, s3, flat(sb), c1, c2, c3, flat(cb), renewed,
        )

    spread = ("dom", "sub")
    rows, all_same, cube = P(spread, None), P(), P(spread, None, None)
    stale = P(None, spread, None)
    in_specs = (
        rows, all_same, rows, rows, rows, rows, cube, cube, cube, P(spread), P(spread), stale, *[all_same] * 12
    )
    out_specs = (*[all_same] * 19, stale)
    return jax.shard_map(local, mesh=mesh, in_specs=in_specs, out_specs=out_specs, check_vma=False)
```

time: 1110 us -> 292 us (0.26)
  waiting for transfers between devices: 506 us -> 0 us
  Pallas kernels: 0 us -> 253 us
  other arithmetic: 210 us -> 5.14 us
  local copies, waits for them, and re-layouts: 198 us -> 32.4 us
  blocking collectives: 82.1 us -> 0 us
  matrix products: 58.1 us -> 0 us
  starting transfers between devices: 24.7 us -> 0 us
  between operations: 19.3 us -> 0.71 us
    psum x4 -> x0, waiting for transfers between devices: 431 us -> none  [the longest x1 131 us: local(): hub_total = lax.psum(table_grad[node_count + halo_count:], ('dom', 'sub'))]
    pallas_call x0 -> x2, Pallas kernels: none -> 253 us  [the longest x1 245 us: train(): pl.pallas_call(functools.partial(train_kernel, z), out_shape=(jax.ShapeDt...]
    gather x14 -> x0, local copies, waits for them, and re-layouts: 176 us -> none  [the longest x9 125 us: one_block(): lookup[block_index]]
    scatter-add x7 -> x0, other arithmetic: 143 us -> none  [the longest x2 90.6 us: local(): table_grad.at[high_lists.reshape(-1)]]
    psum x2 -> x0, blocking collectives: 82.1 us -> none  [the longest x1 41.3 us: local(): lax.psum((weight_grads[0], weight_grads[1], weight_grads[2], jnp.concaten...]
    all_to_all x5 -> x0, waiting for transfers between devices: 74.8 us -> none  [the longest x3 56.6 us: send_forward(): lax.all_to_all(blocks, ('dom', 'sub'), split_axis=0, concat_axis=0, tiled...]
    dot_general x18 -> x0, matrix products: 58.1 us -> none  [the longest x4 18.5 us: one_block(): jnp.einsum('nkf,nk->nf', lookup[block_index], block_weights, precision=pr...]
    all_to_all x5 -> x0, starting transfers between devices: 24 us -> none  [the longest x3 16.5 us: send_forward(): lax.all_to_all(blocks, ('dom', 'sub'), split_axis=0, concat_axis=0, tiled...]
  transfers between devices with their start and end apart: 9 -> 0, of which waited for: 6 -> 0; matrix products, arithmetic and copies ran while one was open for 8% -> 0% of each run, Pallas kernels for 0% -> 0%
where the time goes in v1:
time: 292 us; the launch traced here: 291 us
  Pallas kernels  253 us (87%)
  local copies, waits for them, and re-layouts  32.4 us (11%)
  other arithmetic  5.14 us (2%)
    pallas_call x1, Pallas kernels, train(): pl.pallas_call(functools.partial(train_kernel, z), out_shape=(jax.ShapeDt...  245 us
    unnamed x24, local copies, waits for them, and re-layouts  24.8 us
    pallas_call x1, Pallas kernels, update(): pl.pallas_call(functools.partial(update_kernel, z), out_shape=tuple(shape...  8.02 us

profile of v1, /device:TPU:0, one launch (start us, length us, event | category | flops | bytes accessed | tf_op | source)
XLA Modules:
  0.0 291.2 jit_solution(7016462771210636160)
XLA Ops:
  0.7 0.0 copy-start.3
  0.7 0.0 copy-start.2
  0.7 0.0 copy-start.1
  0.7 1.3 reshape.74.mb
  2.0 1.3 reshape.75.vb
  3.3 1.3 reshape.73.bs
  4.6 0.7 pad.4
  5.2 0.6 reshape.72.bias
  5.9 1.5 copy.48.lowl
  7.3 1.5 copy.49.lowm
  8.8 1.5 copy.50.highl
  10.3 1.5 copy.51.highm
  11.8 1.5 copy.44
  13.3 0.0 copy-start
  13.3 1.6 copy.45
  14.9 1.7 copy.52.w3
  16.6 0.0 copy-done.2
  16.6 0.8 copy.54.m3
  17.4 0.0 copy-done.3
  17.4 0.9 copy.55.v3
  18.3 0.0 copy-done.1
  18.3 1.1 copy.47.hubf
  19.4 0.0 copy-done
  19.4 1.5 copy.46.feat
  20.8 244.9 %train.1 = (f32[2560,128]{1,0:T(8,128)}, f32[1280,128]{1,0:T(8,128)}, f32[2,1024,256]{2,1,0:T(8,128)}, f32[8,128]{1,0:T(8,128)}) custom-call(f32[512,602]{1,0:T(8,128)} %copy.46.feat, f32[256,602]{1,0:T(8,128)} %copy.47.hubf, s32[256,4]{1,0:T(8,128)} %copy.48.lowl, s32[256,4]{1,0:T(8,128)} %copy.49.lowm, s32[256,32]{1,0:T(8,128)} %copy.50.highl, ...), custom_call_target="tpu_custom_call" | custom-call | tf_op jit(solution)/shard_map/train/pallas_call | solution.py:765
  265.7 1.2 slice.6
  266.9 1.3 slice.7
  268.2 8.0 %update.1 = (f32[1,1]{1,0:T(1,128)}, f32[1204,256]{1,0:T(8,128)}, f32[512,256]{1,0:T(8,128)}, f32[512,41]{1,0:T(8,128)}, f32[1,553]{1,0:T(1,128)}, /*index=5*/f3...) custom-call(f32[2560,128]{1,0:T(8,128)} %get-tuple-element.41.early,, ...), custom_call_target="tpu_custom_call" | custom-call | tf_op jit(solution)/shard_map/update/pallas_call | solution.py:841
  276.2 1.3 reduce.3
  277.5 1.3 reduce
  278.8 1.3 reduce.1
  280.1 1.3 reduce.2
  281.3 1.6 copy.59
  283.0 1.7 copy.56
  284.7 1.7 copy.57
  286.4 1.7 copy.58
  288.1 3.0 %copy.61 = f32[2,1024,256]{2,1,0:T(8,128)} copy(f32[2,1024,256]{2,1,0:T(8,128)} %get-tuple-element.121) | data formatting | bytes 4194304
Async XLA Ops:
  0.7 16.8 %copy-start.3 = (f32[512,41]{0,1:T(8,128)S(1)}, f32[512,41]{0,1:T(8,128)}, u32[]{:S(2)}) copy-start(f32[512,41]{0,1:T(8,128)} %param.46) | copy-start | bytes 251908
  0.7 15.9 %copy-start.2 = (f32[512,41]{0,1:T(8,128)S(1)}, f32[512,41]{0,1:T(8,128)}, u32[]{:S(2)}) copy-start(f32[512,41]{0,1:T(8,128)} %param.42) | copy-start | bytes 251908
  0.7 17.6 %copy-start.1 = (f32[256,602]{0,1:T(8,128)S(1)}, f32[256,602]{0,1:T(8,128)}, u32[]{:S(2)}) copy-start(f32[256,602]{0,1:T(8,128)} %param.25) | copy-start | bytes 1849348
  13.3 6.1 %copy-start = (f32[512,602]{0,1:T(8,128)S(1)}, f32[512,602]{0,1:T(8,128)}, u32[]{:S(2)}) copy-start(f32[512,602]{0,1:T(8,128)} %param.24) | copy-start | bytes 3698692

commit v2 on v1

v2 whole, which is shorter than its diff:
```python
import functools

import jax
import jax.numpy as jnp
from jax import lax
from jax.experimental import pallas as pl
from jax.experimental.pallas import tpu as pltpu
from jax.sharding import PartitionSpec as P

MESH = pl.DeviceIdType.MESH
F32 = jnp.float32
BF16 = jnp.bfloat16

STEP = 5
KEEP = 0.95
SMOOTH = 0.1
CLIP = 0.02
RATE = 0.03
DECAY = 0.01
EPSILON = 1e-08
CORRECT = 1.0 - 0.5**STEP
GELU_A = 0.7978845608
GELU_B = 0.044715
LANES = 128


def up(value, unit):
    return -(-value // unit) * unit


def split(values):
    high = values.astype(BF16)
    return high, (values - high.astype(F32)).astype(BF16)


def dot(left, right):
    return jnp.dot(left, right, preferred_element_type=F32)


def dot_nt(left, right):
    return lax.dot_general(left, right, (((1,), (1,)), ((), ())), preferred_element_type=F32)


def dot_tn(left, right):
    return lax.dot_general(left, right, (((0,), (0,)), ((), ())), preferred_element_type=F32)


def three(product, left, right):
    return (
        product(left[0], right[1]) + product(left[1], right[0])
    ) + product(left[0], right[0])


def gelu(v):
    return 0.5 * v * (1.0 + jnp.tanh(GELU_A * (v + GELU_B * (v * v * v))))


def gelu_slope(v):
    t = jnp.tanh(GELU_A * (v + GELU_B * (v * v * v)))
    return 0.5 * (1.0 + t) + (0.5 * GELU_A) * v * (1.0 - t * t) * (1.0 + (3.0 * GELU_B) * (v * v))


def tiles(total, step, body):
    @pl.loop(0, total // step)
    def _(index):
        body(pl.multiple_of(index * step, step))


class Sizes:
    def __init__(self, mesh, features, low_lists, high_lists, hub_lists, send_rows, weight_one, weight_three):
        self.dom, self.sub = mesh.shape["dom"], mesh.shape["sub"]
        self.devices = self.dom * self.sub
        self.nodes, self.fin = features.shape
        self.low, self.k_low = low_lists.shape
        self.high, self.k_high = high_lists.shape
        self.hubs, self.k_hub = hub_lists.shape[1:]
        self.blk = send_rows.shape[2]
        self.halo = self.devices * self.blk
        self.hid = weight_one.shape[1]
        self.halves = self.hid // LANES
        self.cls = weight_three.shape[1]
        self.rows = self.nodes + self.hubs
        self.table = self.nodes + self.halo + self.hubs
        self.fpad = up(self.fin, LANES)
        self.frows = up(self.fin, 8)
        self.shift = self.fin % 8
        self.brows = up(self.fin + self.shift, 8)
        self.part = self.hubs // self.dom
        self.packed = self.blk % 16 == 0
        self.cblk = self.blk // 2 if self.packed else self.blk
        unit = 8 * self.devices
        self.at_three = self.halves * 2 * self.hid
        self.at_bias = self.halves * self.frows
        self.flat = (
            up(self.at_three + self.hid, unit),
            up(self.at_bias + 8, unit),
            up(self.halves * self.brows, unit),
        )
        self.levels = (2, self.dom // 2, self.sub)


class HubSum:
    def __init__(self, z, place, remote, buffers, sems, index):
        self.z, self.place, self.remote = z, place, remote
        self.source, self.ra, self.rb, self.out = buffers
        self.sent, self.got = sems
        self.index = index

    def put(self, values):
        self.source[...] = values.reshape(self.source.shape)

    def sems(self, phase):
        return self.sent.at[self.index, phase], self.got.at[self.index, phase]

    def over_dom(self, start, phase):
        d, s = self.place

        @pl.loop(1, self.z.dom)
        def _(k):
            pd = lax.rem(d + k, self.z.dom)
            src, dst = start(pd)
            self.remote(src, dst, *self.sems(phase), pd, s).start()

    def dom_done(self, ref, phase):
        d, s = self.place
        some = ref.at[pl.ds(0, self.z.dom - 1)]
        copy = self.remote(some, some, *self.sems(phase), lax.rem(d + 1, self.z.dom), s)
        copy.wait_recv()
        copy.wait_send()

    def scatter(self):
        d, s = self.place
        self.over_dom(lambda pd: (self.source.at[pd], self.ra.at[d]), 0)

    def swap(self):
        d, s = self.place
        self.dom_done(self.ra, 0)
        total = self.source[d]
        for k in range(1, self.z.dom):
            total = total + self.ra[lax.rem(d + k, self.z.dom)]
        self.rb[s] = total

        @pl.loop(1, self.z.sub)
        def _(k):
            ps = lax.rem(s + k, self.z.sub)
            self.remote(self.rb.at[s], self.rb.at[s], *self.sems(1), d, ps).start()

    def gather(self):
        d, s = self.place
        some = self.rb.at[pl.ds(0, self.z.sub - 1)]
        copy = self.remote(some, some, *self.sems(1), d, lax.rem(s + 1, self.z.sub))
        copy.wait_recv()
        copy.wait_send()
        total = self.rb[0]
        for k in range(1, self.z.sub):
            total = total + self.rb[k]
        self.out[d] = total
        self.over_dom(lambda pd: (self.out.at[d], self.out.at[d]), 2)

    def end(self):
        self.dom_done(self.out, 2)
        return self.out[...].reshape(self.z.hubs, self.out.shape[-1])


class FlatSum:
    def __init__(self, z, place, remote, buffers, sems, index):
        d, s = place
        self.remote, self.index = remote, index
        self.source, self.out = buffers[0], buffers[1]
        self.landed, self.parts = buffers[2:5], (buffers[0], *buffers[5:7])
        self.sent, self.got = sems
        pair = lax.rem(d, 2)
        chip = d // 2
        self.levels = (
            (2, pair, lambda j: (chip * 2 + j, s)),
            (z.dom // 2, chip, lambda j: (j * 2 + pair, s)),
            (z.sub, s, lambda j: (d, j)),
        )
        self.first, offset, rows = [], 0, self.source.shape[0]
        for size, mine, _ in self.levels:
            rows = rows // size
            self.first.append((offset, rows))
            offset = offset + mine * rows

    def sems(self, phase):
        return self.sent.at[self.index, phase], self.got.at[self.index, phase]

    def rows(self, start, count):
        return pl.ds(pl.multiple_of(start, 8), count)

    def send(self, level):
        size, mine, peer = self.levels[level]
        count = self.first[level][1]

        @pl.loop(1, size)
        def _(k):
            j = lax.rem(mine + k, size)
            self.remote(
                self.parts[level].at[self.rows(j * count, count)],
                self.landed[level].at[mine],
                *self.sems(level),
                *peer(j),
            ).start()

    def receive(self, level):
        size, mine, peer = self.levels[level]
        offset, count = self.first[level]
        ref = self.landed[level]
        some = ref.at[pl.ds(0, size - 1)]
        copy = self.remote(some, some, *self.sems(level), *peer(lax.rem(mine + 1, size)))
        copy.wait_recv()
        copy.wait_send()
        total = self.parts[level][self.rows(mine * count, count), :]
        for k in range(1, size):
            total = total + ref[lax.rem(mine + k, size)]
        if level + 1 < len(self.levels):
            self.parts[level + 1][...] = total
        else:
            self.out[self.rows(offset + mine * count, count), :] = total

    def spread(self, level):
        size, mine, peer = self.levels[level]
        offset, count = self.first[level]
        held = self.out.at[self.rows(offset + mine * count, count)]

        @pl.loop(1, size)
        def _(k):
            j = lax.rem(mine + k, size)
            self.remote(held, held, *self.sems(3 + level), *peer(j)).start()

    def collect(self, level):
        size, mine, peer = self.levels[level]
        some = self.out.at[pl.ds(0, (size - 1) * self.first[level][1])]
        copy = self.remote(some, some, *self.sems(3 + level), *peer(lax.rem(mine + 1, size)))
        copy.wait_recv()
        copy.wait_send()


HUB_SUMS = (1, 1, 1, 1, 1, 1, 2)


def train_kernel(
    z,
    feat, hubf, lowl, lowm, highl, highm, hubl, hubm, send, lab, tmask, stale_hbm, w1, w2, w3, bias,
    two_hbm, upper_hbm, lower_hbm, fresh_hbm, misc,
    ab, abt, sel, selt, colb, keyt, keys, xh, xl, xth, xtl, w1h, w1l, w2h, w2l, w3t, w3h, w3l,
    tb, tc, inv, q, magg, h1h, h1l, m1h, m1l, h2h, h2l, dg0, dg1, dph, dpl, dmh, dml, eb, gown, gthree, stale,
    zst, pself, labc, trainw, brow,
    send_a, recv_a, send_b, recv_b, send_c, recv_c, send_d, recv_d, recv_e, recv_f, send_g, recv_g,
    *rest_refs,
):
    hub_refs, flat_refs = rest_refs[: 4 * len(HUB_SUMS)], rest_refs[4 * len(HUB_SUMS) : -7]
    xs, xr, hsem_s, hsem_r, gsem_s, gsem_r, lsem = rest_refs[-7:]
    send_e, send_f = send_a, send_b
    d = lax.axis_index("dom")
    s = lax.axis_index("sub")
    me = d * z.sub + s
    nd, halo, hubs, hid, fin = z.nodes, z.halo, z.hubs, z.hid, z.fin
    halo0, hub0 = nd, nd + halo
    own, halos, hubr = slice(0, nd), slice(halo0, hub0), slice(hub0, z.table)
    hubq = slice(nd, z.rows)
    up_rows, low_rows = slice(0, hid), slice(hid, 2 * hid)
    i32 = jnp.int32
    both = range(z.halves)

    def lanes(h):
        return slice(h * LANES, (h + 1) * LANES)

    barrier = pltpu.get_barrier_semaphore()

    @pl.loop(1, z.devices)
    def _(k):
        pl.semaphore_signal(
            barrier,
            inc=1,
            device_id=(lax.rem(d + k // z.sub, z.dom), lax.rem(s + k % z.sub, z.sub)),
            device_id_type=MESH,
        )

    stale_copy = pltpu.make_async_copy(stale_hbm, stale, lsem.at[0])
    stale_copy.start()

    def remote(src, dst, ssem, rsem, pd, ps):
        return pltpu.make_async_remote_copy(
            src_ref=src, dst_ref=dst, send_sem=ssem, recv_sem=rsem, device_id=(pd, ps), device_id_type=MESH
        )

    place = (d, s)
    sums = [
        HubSum(z, place, remote, hub_refs[4 * i : 4 * i + 4], (hsem_s, hsem_r), i) for i in range(len(HUB_SUMS))
    ]
    grads = [FlatSum(z, place, remote, flat_refs[7 * i : 7 * i + 7], (gsem_s, gsem_r), i) for i in range(3)]
    two, upper, lower = grads

    def part_of(portion):
        return 1 + (z.devices - 1) * portion // 8

    def exchange_start(src, dst, i, first=0, last=8):
        @pl.loop(part_of(first), part_of(last))
        def _(k):
            pd = lax.rem(d + k // z.sub, z.dom)
            ps = lax.rem(s + k % z.sub, z.sub)
            remote(src.at[pd * z.sub + ps], dst.at[me], xs.at[i], xr.at[i], pd, ps).start()

        if first == 0:
            dst[me] = src[me]

    def exchange_wait(src, dst, i):
        some = pl.ds(0, z.devices - 1)
        copy = remote(src.at[some], dst.at[some], xs.at[i], xr.at[i], lax.rem(d + 1, z.dom), s)
        copy.wait_recv()
        copy.wait_send()

    def put_split(ref, rows, values):
        width = values.shape[1]
        high, rest = split(values)
        ref[rows, 0:width] = high
        ref[rows, width : 2 * width] = rest

    def put_pair(high_ref, rest_ref, rows, columns, values):
        high, rest = split(values)
        high_ref[rows, columns] = high
        rest_ref[rows, columns] = rest
        return high, rest

    def added(product):
        return product[:, :LANES] + product[:, LANES:]

    per_tile = 256 // z.blk

    keyt[...] = jnp.full(keyt.shape, -1, i32)
    keyt[0 : z.k_low, 0 : z.low] = jnp.where(lowm[...] > 0, lowl[...], -1)
    keyt[0 : z.k_high, z.low : nd] = jnp.where(highm[...] > 0, highl[...], -1)
    keyt[0 : z.k_hub, hubq] = jnp.where(hubm[...] > 0, hubl[...], -1)
    for block in range(z.rows // LANES):
        keys[lanes(block), :] = keyt[:, lanes(block)].T
    counts = jnp.sum(jnp.where(keys[...] >= 0, 1.0, 0.0), axis=1, keepdims=True)
    inv[own, :] = 1.0 / jnp.maximum(counts[own, :], 1.0)
    train_local = jnp.sum(jnp.sum(tmask[...].astype(F32), axis=1, keepdims=True), axis=0, keepdims=True)
    lane = lax.broadcasted_iota(i32, (hubs, LANES), 1)
    sums[0].put(jnp.where(lane == 0, counts[hubq, :], jnp.where(lane == 1, train_local, 0.0)))

    def turn(source, target, r_count, c_count, c_start=0, step=128):
        def body(r):
            for c in range(c_start, c_count, step):
                target[c : c + step, pl.ds(r, step)] = source[pl.ds(r, step), c : c + step].T

        tiles(r_count, step, body)

    pad0 = fin // 16 * 16
    xth[pad0 : z.fpad, :] = jnp.zeros((z.fpad - pad0, z.rows), BF16)
    xtl[pad0 : z.fpad, :] = jnp.zeros((z.fpad - pad0, z.rows), BF16)
    w1h[pad0 : z.fpad, :] = jnp.zeros((z.fpad - pad0, 2 * hid), BF16)
    w1l[pad0 : z.fpad, :] = jnp.zeros((z.fpad - pad0, 2 * hid), BF16)
    put_pair(xth, xtl, slice(0, fin), own, feat[...])
    turn(xth, xh, z.fpad, nd)
    turn(xtl, xl, z.fpad, nd)
    pl.semaphore_wait(barrier, z.devices - 1)
    sums[0].scatter()
    put_pair(w1h, w1l, slice(0, fin), low_rows, w1[fin : 2 * fin, :])

    def project(rows, columns):
        return three(dot, (xh[rows, :], xl[rows, :]), (w1h[:, columns], w1l[:, columns]))

    def put_halves(rows, values):
        for h in both:
            put_split(tb.at[h], rows, values[:, lanes(h)])

    tiles(nd, 256, lambda r: put_halves(pl.ds(r, 256), project(pl.ds(r, 256), low_rows)))
    sums[0].swap()

    eye = lax.broadcasted_iota(i32, (z.blk, z.blk), 0) == lax.broadcasted_iota(i32, (z.blk, z.blk), 1)

    @pl.loop(0, z.devices)
    def _(p):
        line = jnp.broadcast_to(send[pl.ds(p, 1), :], (z.blk, z.blk))
        colb[pl.ds(pl.multiple_of(p * z.blk, z.blk), z.blk), :] = jnp.sum(
            jnp.where(eye, line, 0), axis=1, keepdims=True
        )

    def sel_tile(r):
        rows = pl.ds(r, 256)
        sel[rows, :] = jnp.where(colb[rows, :] == lax.broadcasted_iota(i32, (256, nd), 1), 1.0, 0.0).astype(BF16)

    tiles(halo, 256, sel_tile)

    def pick(source, target):
        def body(r):
            values = added(dot(sel[pl.ds(r, 256), :], source[own, :]))
            target[pl.ds(r // z.blk, per_tile)] = values.reshape(per_tile, z.blk, LANES)

        tiles(halo, 256, body)

    pick(tb.at[0], send_a.at[0])
    sums[0].gather()
    for h in both:
        if h:
            pick(tb.at[h], send_a.at[h])
        exchange_start(send_a.at[h], recv_a.at[h], h)

    def build(first, count, slots):
        width = z.table // 2

        def group(r):
            rows = pl.ds(first + r, 16)
            key = keys[rows, :]
            for half in range(2):
                spot = lax.broadcasted_iota(i32, (16, width), 1) + half * width
                total = jnp.zeros((16, width), F32)
                for k in range(slots):
                    total = total + jnp.where(key[:, k : k + 1] == spot, 1.0, 0.0)
                ab[rows, half * width : (half + 1) * width] = total.astype(BF16)

        tiles(count, 16, group)

    build(0, z.low, z.k_low)
    build(nd, hubs, z.k_hub)
    hub_totals = sums[0].end()
    inv[hubq, :] = 1.0 / hub_totals[:, 0:1]
    misc[...] = hub_totals[0:8, :]
    build(z.low, z.high, z.k_high)

    put_pair(xth, xtl, slice(0, fin), hubq, hubf[...])
    turn(xth, xh, z.fpad, z.rows, nd)
    turn(xtl, xl, z.fpad, z.rows, nd)
    put_pair(w1h, w1l, slice(0, fin), up_rows, w1[0:fin, :])
    brow[...] = jnp.zeros(brow.shape, F32)
    line = bias[...].reshape(1, 2 * hid + z.cls)
    brow[0:1, :] = line[:, 0:hid]
    brow[1:2, :] = line[:, hid : 2 * hid]
    brow[2:3, 0 : z.cls] = line[:, 2 * hid : 2 * hid + z.cls]
    put_halves(hubr, project(hubq, low_rows))

    def own_tile(r):
        rows = pl.ds(r, 256)
        q[rows, :] = project(rows, up_rows) + brow[0:1, :]

    tiles(z.rows, 256, own_tile)

    def gather_local(h):
        def body(r):
            rows = pl.ds(r, 256)
            magg[rows, lanes(h)] = added(dot(ab[rows, own], tb[h, own, :]) + dot(ab[rows, hubr], tb[h, hubr, :]))

        tiles(z.rows, 256, body)

    for h in both:
        gather_local(h)
    put_pair(w2h, w2l, slice(0, 2 * hid), slice(0, hid), w2[...])
    w3t[...] = jnp.zeros(w3t.shape, F32)
    w3t[0 : z.cls, :] = w3[...]
    put_pair(w3h, w3l, slice(0, 2 * hid), slice(0, LANES), w3t[...].T)

    def with_halo(rows, h):
        return magg[rows, lanes(h)] + added(dot(ab[rows, halos], tb[h, halos, :]))

    def layer_one(h):
        def body(r):
            rows = pl.ds(r, 256)
            pre = q[rows, lanes(h)] + with_halo(rows, h) * inv[rows, :]
            q[rows, lanes(h)] = pre
            high, rest = put_pair(h1h, h1l, rows, lanes(h), gelu(pre))
            tb[h, rows, 0:LANES] = high
            tb[h, rows, LANES : 2 * LANES] = rest

        tiles(nd, 256, body)

    def first_half():
        exchange_wait(send_a.at[0], recv_a.at[0], 0)
        put_split(tb.at[0], halos, recv_a[0].reshape(halo, LANES))
        sums[1].put(with_halo(hubq, 0))
        sums[1].scatter()
        layer_one(0)
        pick(tb.at[0], send_b.at[0])
        exchange_start(send_b.at[0], recv_b.at[0], 2, 0, 4)

    first_half()
    exchange_wait(send_a.at[1], recv_a.at[1], 1)
    sums[1].swap()
    put_split(tb.at[1], halos, recv_a[1].reshape(halo, LANES))
    sums[2].put(with_halo(hubq, 1))
    sums[2].scatter()
    exchange_start(send_b.at[0], recv_b.at[0], 2, 4, 8)
    layer_one(1)
    pick(tb.at[1], send_b.at[1])
    sums[1].gather()
    sums[2].swap()
    exchange_start(send_b.at[1], recv_b.at[1], 3, 0, 4)
    turn(ab, abt, z.rows, z.table)
    sums[2].gather()
    exchange_start(send_b.at[1], recv_b.at[1], 3, 4, 8)

    turn(sel, selt, halo, nd)
    stale_copy.wait()
    zst[...] = three(dot, split(KEEP * stale[1]), (w3h[low_rows, :], w3l[low_rows, :]))
    dg0[own, :] = gelu_slope(q[own, :])
    for block in range(nd // LANES):
        diag = lax.broadcasted_iota(i32, (LANES, LANES), 0) == lax.broadcasted_iota(i32, (LANES, LANES), 1)
        line = jnp.broadcast_to(lab[block : block + 1, :], (LANES, LANES))
        labc[lanes(block), :] = jnp.sum(jnp.where(diag, line, 0), axis=1, keepdims=True)
        line = jnp.broadcast_to(tmask[block : block + 1, :].astype(F32), (LANES, LANES))
        trainw[lanes(block), :] = jnp.sum(jnp.where(diag, line, 0.0), axis=1, keepdims=True)
    for h in both:
        pre = q[hubq, lanes(h)] + sums[1 + h].end() * inv[hubq, :]
        dg0[hubq, lanes(h)] = gelu_slope(pre)
        high, rest = put_pair(h1h, h1l, hubq, lanes(h), gelu(pre))
        tb[h, hubr, 0:LANES] = high
        tb[h, hubr, LANES : 2 * LANES] = rest

    for h in both:
        gather_local(h)

    def own_two(r):
        rows = pl.ds(r, 256)
        q[rows, :] = three(dot, (h1h[rows, :], h1l[rows, :]), (w2h[up_rows, :], w2l[up_rows, :])) + brow[1:2, :]

    tiles(z.rows, 256, own_two)

    def second(h):
        exchange_wait(send_b.at[h], recv_b.at[h], 2 + h)
        renewed = KEEP * stale[0, :, lanes(h)] + (1.0 - KEEP) * recv_b[h].reshape(halo, LANES)
        stale[0, :, lanes(h)] = renewed
        put_split(tb.at[h], halos, renewed)
        sums[3 + h].put(with_halo(hubq, h))
        sums[3 + h].scatter()

        def body(r):
            rows = pl.ds(r, 256)
            put_pair(m1h, m1l, rows, lanes(h), with_halo(rows, h) * inv[rows, :])

        tiles(nd, 256, body)

    second(0)
    sums[3].swap()
    second(1)
    sums[3].gather()

    def layer_two(r):
        rows = pl.ds(r, 256)
        pre = q[rows, :] + three(dot, (m1h[rows, :], m1l[rows, :]), (w2h[low_rows, :], w2l[low_rows, :]))
        q[rows, :] = pre
        high, rest = put_pair(h2h, h2l, rows, slice(0, hid), gelu(pre))
        put_split(tc, rows, three(dot, (high, rest), (w3h[low_rows, :], w3l[low_rows, :])))

    tiles(nd, 256, layer_two)
    class_lane = lax.broadcasted_iota(i32, (1, 1, LANES), 2) < LANES // 2

    def pack(values):
        blocks = values.reshape(values.shape[0] // z.blk, z.blk, LANES)
        if z.packed:
            return blocks[:, : z.cblk] + pltpu.roll(blocks[:, z.cblk :], LANES // 2, 2)
        return blocks

    def unpack(blocks):
        if z.packed:
            first = jnp.where(class_lane, blocks, 0.0)
            second = jnp.where(class_lane, pltpu.roll(blocks, LANES // 2, 2), 0.0)
            blocks = jnp.concatenate([first, second], axis=1)
        return blocks.reshape(halo, LANES)

    def pick_class(r):
        send_c[pl.ds(r // z.blk, per_tile)] = pack(added(dot(sel[pl.ds(r, 256), :], tc[own, :])))

    tiles(halo, 256, pick_class)
    sums[4].swap()
    exchange_start(send_c, recv_c, 4)

    def pick_wide(r):
        chosen = sel[pl.ds(r, 256), :]
        values = dot(chosen, h2l[own, :]) + dot(chosen, h2h[own, :])
        send_g[pl.ds(r // z.blk, per_tile)] = values.reshape(per_tile, z.blk, hid)

    tiles(halo, 256, pick_wide)
    sums[4].gather()
    exchange_start(send_g, recv_g, 5, 0, 3)

    def own_three(r):
        rows = pl.ds(r, 256)
        pself[rows, :] = three(dot, (h2h[rows, :], h2l[rows, :]), (w3h[up_rows, :], w3l[up_rows, :])) + brow[2:3, 0:LANES]

    tiles(nd, 256, own_three)
    dg1[own, :] = gelu_slope(q[own, :])
    for h in both:
        put_pair(m1h, m1l, hubq, lanes(h), sums[3 + h].end() * inv[hubq, :])
    pre = q[hubq, :] + three(dot, (m1h[hubq, :], m1l[hubq, :]), (w2h[low_rows, :], w2l[low_rows, :]))
    high, rest = put_pair(h2h, h2l, hubq, slice(0, hid), gelu(pre))
    put_split(tc, hubr, three(dot, (high, rest), (w3h[low_rows, :], w3l[low_rows, :])))
    q[hubq, :] = pre

    def class_local(r):
        rows = pl.ds(r, 256)
        magg[rows, 0:LANES] = added(dot(ab[rows, own], tc[own, :]) + dot(ab[rows, hubr], tc[hubr, :]))

    tiles(nd, 256, class_local)

    two.source[...] = jnp.zeros(two.source.shape, F32)
    upper.source[...] = jnp.zeros(upper.source.shape, F32)
    lower.source[...] = jnp.zeros(lower.source.shape, F32)
    exchange_wait(send_c, recv_c, 4)
    put_split(tc, halos, zst[...] + (1.0 - KEEP) * unpack(recv_c[...]))
    used = lax.broadcasted_iota(i32, (256, LANES), 1)
    train_total = misc[0:1, 1:2]
    at_bias = z.at_bias

    def head(r):
        rows = pl.ds(r, 256)
        logits = pself[rows, :] + (magg[rows, 0:LANES] + added(dot(ab[rows, halos], tc[halos, :]))) * inv[rows, :]
        valid = used < z.cls
        top = jnp.max(jnp.where(valid, logits, -1e30), axis=1, keepdims=True)
        shifted = logits - top
        powers = jnp.where(valid, jnp.exp(jnp.where(valid, shifted, 0.0)), 0.0)
        total = jnp.sum(powers, axis=1, keepdims=True)
        log_probs = jnp.where(valid, shifted - jnp.log(total), 0.0)
        target = jnp.where(used == labc[rows, :], 1.0 - SMOOTH, 0.0) + SMOOTH / z.cls
        weight = trainw[rows, :]
        losses = jnp.sum(jnp.where(valid, -target * log_probs, 0.0), axis=1, keepdims=True) * weight
        grad = jnp.where(valid, powers / total - target, 0.0) * weight / train_total
        at = at_bias + 2 * z.halves
        upper.source[at : at + 1, :] = upper.source[at : at + 1, :] + jnp.sum(grad, axis=0, keepdims=True)
        at = at + 1
        upper.source[at : at + 1, :] = upper.source[at : at + 1, :] + jnp.sum(losses, axis=0, keepdims=True)
        put_pair(dph, dpl, rows, slice(0, LANES), grad)
        put_split(eb.at[0], rows, grad * inv[rows, :])

    tiles(nd, 256, head)

    sums[5].put(added(dot(abt[hubr, own], eb[0, own, :])))
    sums[5].scatter()

    def back_class(r):
        values = added(dot(abt[pl.ds(halo0 + r, 256), own], eb[0, own, :]))
        put_split(tc, pl.ds(halo0 + r, 256), values)
        send_d[pl.ds(r // z.blk, per_tile)] = pack((1.0 - KEEP) * values)

    tiles(halo, 256, back_class)
    sums[5].swap()
    exchange_start(send_d, recv_d, 6)
    gown[own, 0:LANES] = added(dot(abt[own, own], eb[0, own, :]))

    gthree[:, 0:LANES] = three(dot_tn, split(KEEP * stale[1]), (tc[halos, 0:LANES], tc[halos, LANES : 2 * LANES]))
    sums[5].gather()
    exchange_start(send_g, recv_g, 5, 3, 6)
    hub_class = split(sums[5].source[...].reshape(hubs, LANES))
    gthree[:, 0:LANES] = gthree[:, 0:LANES] + three(dot_tn, (h2h[hubq, :], h2l[hubq, :]), hub_class)
    gthree[:, LANES : 2 * LANES] = three(dot_tn, (h2h[own, :], h2l[own, :]), (dph[own, 0:LANES], dpl[own, 0:LANES]))
    dg1[hubq, :] = gelu_slope(q[hubq, :])

    def self_two(r):
        rows = pl.ds(r, 256)
        magg[rows, :] = three(
            dot_nt, (dph[rows, 0:LANES], dpl[rows, 0:LANES]), (w3h[up_rows, :], w3l[up_rows, :])
        )

    tiles(nd, 256, self_two)

    def owned(values):
        row = lax.broadcasted_iota(i32, (hubs, 1), 0)
        share = hubs // z.devices
        mine = jnp.where(row >= me * share, 1.0, 0.0) * jnp.where(row < (me + 1) * share, 1.0, 0.0)
        return values * mine

    def column_sums(columns):
        return jnp.sum(dmh[:, columns].astype(F32) + dml[:, columns].astype(F32), axis=0, keepdims=True)

    node = three(dot_nt, split(sums[5].end()), (w3h[low_rows, :], w3l[low_rows, :])) * dg1[hubq, :]
    put_pair(dph, dpl, hubq, slice(0, hid), node)
    put_pair(dmh, dml, hubq, slice(0, hid), owned(node))

    def spread(rows):
        values = three(dot_nt, (dph[rows, :], dpl[rows, :]), (w2h[low_rows, :], w2l[low_rows, :])) * inv[rows, :]
        for h in both:
            put_split(eb.at[h], rows, values[:, lanes(h)])

    spread(hubq)
    exchange_wait(send_d, recv_d, 6)
    put_split(tc, halos, unpack(recv_d[...]))

    def back_two(r):
        rows = pl.ds(r, 256)
        own_class = gown[rows, 0:LANES] + added(dot(selt[rows, :], tc[halos, :]))
        gown[rows, 0:LANES] = own_class
        node = (
            three(dot_nt, split(own_class), (w3h[low_rows, :], w3l[low_rows, :])) + magg[rows, :]
        ) * dg1[rows, :]
        high, rest = put_pair(dph, dpl, rows, slice(0, hid), node)
        dmh[rows, :] = high
        dml[rows, :] = rest
        spread(rows)

    tiles(nd, 256, back_two)

    for h in both:
        sums[6].source[:, :, lanes(h)] = added(dot(abt[hubr, :], eb[h])).reshape(z.dom, z.part, LANES)
    sums[6].scatter()

    def send_halo(target, factor, h):
        def body(r):
            values = added(dot(abt[pl.ds(halo0 + r, 256), :], eb[h])) * factor
            target[pl.ds(r // z.blk, per_tile)] = values.reshape(per_tile, z.blk, LANES)

        tiles(halo, 256, body)

    send_halo(send_e.at[0], 1.0 - KEEP, 0)
    exchange_start(send_e.at[0], recv_e.at[0], 7, 0, 4)
    sums[6].swap()
    exchange_start(send_e.at[0], recv_e.at[0], 7, 4, 8)
    send_halo(send_e.at[1], 1.0 - KEEP, 1)
    sums[6].gather()
    exchange_start(send_e.at[1], recv_e.at[1], 8, 0, 4)

    def own_back(r):
        rows = pl.ds(r, 256)
        q[rows, :] = three(dot_nt, (dph[rows, :], dpl[rows, :]), (w2h[up_rows, :], w2l[up_rows, :]))

    tiles(z.rows, 256, own_back)

    def own_table(r):
        rows = pl.ds(r, 256)
        for h in both:
            q[rows, lanes(h)] = q[rows, lanes(h)] + added(dot(abt[rows, :], eb[h]))

    tiles(nd, 256, own_table)
    gthree[:, 0:LANES] = gthree[:, 0:LANES] + three(dot_tn, (h2h[own, :], h2l[own, :]), split(gown[own, 0:LANES]))
    two.source[z.at_three : z.at_three + hid, :] = gthree[:, LANES : 2 * LANES] + pltpu.roll(
        gthree[:, 0:LANES], LANES // 2, 1
    )
    for h in both:
        start = h * 2 * hid
        pair = (dmh[:, lanes(h)], dml[:, lanes(h)])
        two.source[start : start + hid, :] = three(dot_tn, (h1h[...], h1l[...]), pair)
        two.source[start + hid : start + 2 * hid, :] = three(dot_tn, (m1h[...], m1l[...]), pair)
        at = at_bias + z.halves + h
        upper.source[at : at + 1, :] = column_sums(lanes(h))
    two.send(0)
    exchange_start(send_e.at[1], recv_e.at[1], 8, 4, 8)

    node = (sums[6].end() + q[hubq, :]) * dg0[hubq, :]
    put_pair(dmh, dml, hubq, slice(0, hid), owned(node))
    node = node * inv[hubq, :]
    for h in both:
        put_split(eb.at[h], hubq, node[:, lanes(h)])

    def back_one(h):
        exchange_wait(send_e.at[h], recv_e.at[h], 7 + h)
        put_split(tb.at[h], halos, recv_e[h].reshape(halo, LANES))

        def body(r):
            rows = pl.ds(r, 256)
            node = (q[rows, lanes(h)] + added(dot(selt[rows, :], tb[h, halos, :]))) * dg0[rows, lanes(h)]
            put_pair(dmh, dml, rows, lanes(h), node)
            put_split(eb.at[h], rows, node * inv[rows, :])

        tiles(nd, 256, body)
        send_halo(send_f.at[h], 1.0, h)

    back_one(0)
    exchange_start(send_f.at[0], recv_f.at[0], 9)
    two.receive(0)
    two.send(1)
    back_one(1)
    exchange_start(send_f.at[1], recv_f.at[1], 10, 0, 4)
    two.receive(1)
    two.send(2)
    for h in both:
        top = three(dot, (xth[...], xtl[...]), (dmh[:, lanes(h)], dml[:, lanes(h)]))
        upper.source[h * z.frows : (h + 1) * z.frows, :] = top[0 : z.frows, :]
        upper.source[at_bias + h : at_bias + h + 1, :] = column_sums(lanes(h))
    upper.send(0)
    exchange_start(send_f.at[1], recv_f.at[1], 10, 4, 8)
    two.receive(2)
    two.spread(2)

    def own_last(r):
        rows = pl.ds(r, 256)
        for h in both:
            gown[rows, lanes(h)] = added(dot(abt[rows, :], eb[h]))

    tiles(nd, 256, own_last)
    for h in both:
        put_pair(dmh, dml, hubq, lanes(h), added(dot(abt[hubr, :], eb[h])))
    upper.receive(0)
    upper.send(1)
    two.collect(2)
    two.spread(1)

    def last(h):
        exchange_wait(send_f.at[h], recv_f.at[h], 9 + h)
        put_split(tb.at[h], halos, recv_f[h].reshape(halo, LANES))

        def body(r):
            rows = pl.ds(r, 256)
            put_pair(dmh, dml, rows, lanes(h), gown[rows, lanes(h)] + added(dot(selt[rows, :], tb[h, halos, :])))

        tiles(nd, 256, body)
        bottom = three(dot, (xth[...], xtl[...]), (dmh[:, lanes(h)], dml[:, lanes(h)]))
        start = h * z.brows + z.shift
        lower.source[start : start + fin, :] = bottom[0:fin, :]

    last(0)
    two.collect(1)
    two.spread(0)
    upper.receive(1)
    upper.send(2)
    last(1)
    lower.send(0)
    exchange_start(send_g, recv_g, 5, 6, 8)
    upper.receive(2)
    upper.spread(2)
    two.collect(0)
    two_copy = pltpu.make_async_copy(two.out, two_hbm, lsem.at[1])
    two_copy.start()
    lower.receive(0)
    lower.send(1)
    upper.collect(2)
    upper.spread(1)
    lower.receive(1)
    lower.send(2)
    upper.collect(1)
    upper.spread(0)
    lower.receive(2)
    lower.spread(2)
    exchange_wait(send_g, recv_g, 5)
    stale[1] = KEEP * stale[1] + (1.0 - KEEP) * recv_g[...].reshape(halo, hid)
    fresh_copy = pltpu.make_async_copy(stale, fresh_hbm, lsem.at[2])
    fresh_copy.start()
    lower.collect(2)
    lower.spread(1)
    upper.collect(0)
    upper_copy = pltpu.make_async_copy(upper.out, upper_hbm, lsem.at[3])
    upper_copy.start()
    lower.collect(1)
    lower.spread(0)
    lower.collect(0)
    lower_copy = pltpu.make_async_copy(lower.out, lower_hbm, lsem.at[4])
    lower_copy.start()
    two_copy.wait()
    fresh_copy.wait()
    upper_copy.wait()
    lower_copy.wait()


def train(z, *args):
    b, f, i = BF16, F32, jnp.int32
    vmem = pltpu.VMEM
    n, rows, tab, hid, halo = z.nodes, z.rows, z.table, z.hid, z.halo
    wide = (z.halves, z.devices, z.blk, LANES)
    bulk = (z.devices, z.blk, hid)
    thin = (z.devices, z.cblk, LANES)

    def hub_buffers(count):
        width = count * LANES
        return [
            vmem((z.dom, z.part, width), f),
            vmem((z.dom, z.part, width), f),
            vmem((z.sub, z.part, width), f),
            vmem((z.dom, z.part, width), f),
        ]

    def flat_buffers(total):
        landed, parts, rest = [], [], total
        for size in z.levels:
            rest = rest // size
            landed.append(vmem((size, rest, LANES), f))
            parts.append(vmem((rest, LANES), f))
        return [vmem((total, LANES), f), vmem((total, LANES), f), *landed, *parts[:2]]

    def pairs(count, *shape):
        return [vmem(shape, b) for _ in range(2 * count)]

    scratch = [
        vmem((rows, tab), b), vmem((tab, rows), b), vmem((halo, n), b), vmem((n, halo), b), vmem((halo, 1), i),
        vmem((LANES, rows), i), vmem((rows, LANES), i),
        *pairs(1, rows, z.fpad), *pairs(1, z.fpad, rows), *pairs(1, z.fpad, 2 * hid), *pairs(1, 2 * hid, hid),
        vmem((LANES, 2 * hid), f), *pairs(1, 2 * hid, LANES),
        vmem((z.halves, tab, 2 * LANES), b), vmem((tab, 2 * LANES), b), vmem((rows, 1), f), vmem((rows, hid), f),
        vmem((rows, hid), f),
        *pairs(3, rows, hid),
        vmem((rows, hid), f), vmem((rows, hid), f),
        *pairs(2, rows, hid),
        vmem((z.halves, rows, 2 * LANES), b), vmem((n, hid), f), vmem((hid, 2 * LANES), f),
        vmem((2, halo, hid), f),
        vmem((halo, LANES), f), vmem((n, LANES), f), vmem((n, 1), i), vmem((n, 1), f), vmem((8, hid), f),
        *[vmem(shape, f) for shape in (wide, wide, wide, wide, thin, thin, thin, thin, wide, wide, bulk, bulk)],
    ]
    for count in HUB_SUMS:
        scratch += hub_buffers(count)
    for total in z.flat:
        scratch += flat_buffers(total)
    dma = pltpu.SemaphoreType.DMA
    scratch += [
        dma((11,)), dma((11,)), dma((len(HUB_SUMS), 3)), dma((len(HUB_SUMS), 3)), dma((3, 6)), dma((3, 6)), dma((5,))
    ]
    inside = pl.BlockSpec(memory_space=pltpu.VMEM)
    outside = pl.BlockSpec(memory_space=pl.ANY)
    return pl.pallas_call(
        functools.partial(train_kernel, z),
        out_shape=(
            *[jax.ShapeDtypeStruct((total, LANES), f) for total in z.flat],
            jax.ShapeDtypeStruct((2, halo, hid), f),
            jax.ShapeDtypeStruct((8, LANES), f),
        ),
        in_specs=[inside] * 11 + [outside] + [inside] * 4,
        out_specs=(outside, outside, outside, outside, inside),
        scratch_shapes=scratch,
        compiler_params=pltpu.CompilerParams(
            collective_id=0, has_side_effects=True, vmem_limit_bytes=62 * 1024 * 1024
        ),
        name="train",
    )(*args)


def update_kernel(z, two, upper, lower, misc, fresh, w1, w2, w3, bs, m1, m2, m3, mb, v1, v2, v3, vb,
                  o_norm, o_loss, o_count, o_fresh, o1, o2, o3, ob, n1, n2, n3, nb, s1, s2, s3, sb, c1, c2, c3, cb,
                  held, sem):
    taken = pltpu.make_async_copy(fresh, held, sem.at[0])
    taken.start()

    def squares(values):
        return jnp.sum(jnp.sum(values * values, axis=0, keepdims=True), axis=1, keepdims=True)

    at_loss = z.at_bias + 2 * z.halves + 1
    norm = jnp.sqrt(squares(two[...]) + squares(upper[0:at_loss, :]) + squares(lower[...]))
    o_norm[...] = norm
    o_loss[...] = upper[at_loss : at_loss + 1, 0:1]
    o_count[...] = misc[0:1, 1:2]
    factor = jnp.minimum(1.0, CLIP / (norm + 1e-06))

    def renew(rows, lanes, grad, w, m, v, ow, om, ov, oc=None):
        clipped = grad * factor
        moment = 0.5 * m[rows, lanes] + 0.5 * clipped
        second = 0.5 * v[rows, lanes] + 0.5 * clipped * clipped
        old = w[rows, lanes]
        om[rows, lanes] = moment
        ov[rows, lanes] = second
        fresh_weight = old - RATE * ((moment / CORRECT) / (jnp.sqrt(second / CORRECT) + EPSILON) + DECAY * old)
        ow[rows, lanes] = fresh_weight
        if oc is not None:
            oc[rows, lanes] = fresh_weight.astype(BF16)

    taken.wait()
    moved = pltpu.make_async_copy(held, o_fresh, sem.at[1])
    moved.start()
    low = z.fin - z.shift
    for half in range(z.halves):
        lanes = slice(half * LANES, (half + 1) * LANES)
        u0, l0 = half * z.frows, half * z.brows
        one = (w1, m1, v1, o1, n1, s1)
        renew(slice(0, low), lanes, upper[u0 : u0 + low, :], *one)
        if z.shift:
            renew(slice(low, low + 8), lanes, upper[u0 + low : u0 + low + 8, :] + lower[l0 : l0 + 8, :], *one)
            renew(slice(low + 8, 2 * z.fin), lanes, lower[l0 + 8 : l0 + z.fin + z.shift, :], *one)
        else:
            renew(slice(low, 2 * z.fin), lanes, lower[l0 : l0 + z.fin, :], *one)
        start = half * 2 * z.hid
        renew(slice(0, 2 * z.hid), lanes, two[start : start + 2 * z.hid, :], w2, m2, v2, o2, n2, s2, c2)
    packed = two[z.at_three : z.at_three + z.hid, :].T
    for half in range(2):
        grad = packed[half * (LANES // 2) : half * (LANES // 2) + z.cls, :]
        renew(slice(0, z.cls), slice(half * z.hid, (half + 1) * z.hid), grad, w3, m3, v3, o3, n3, s3, c3)
    c1[...] = o1[...].astype(BF16)
    size = bs.shape[0]
    line = jnp.concatenate([upper[z.at_bias + k : z.at_bias + k + 1, :] for k in range(2 * z.halves + 1)], axis=1)
    clipped = line[:, 0:size] * factor
    flat = lambda ref: ref[...].reshape(1, size)
    moment = 0.5 * flat(mb) + 0.5 * clipped
    second = 0.5 * flat(vb) + 0.5 * clipped * clipped
    old = flat(bs)
    fresh_bias = old - RATE * ((moment / CORRECT) / (jnp.sqrt(second / CORRECT) + EPSILON) + DECAY * old)
    ob[...] = fresh_bias.reshape(size)
    nb[...] = moment.reshape(size)
    sb[...] = second.reshape(size)
    cb[...] = ob[...].astype(BF16)
    moved.wait()


def update(z, *args):
    weights = args[5:9]
    same = [jax.ShapeDtypeStruct(w.shape, F32) for w in weights]
    copies = [jax.ShapeDtypeStruct(w.shape, BF16) for w in weights]
    inside = pl.BlockSpec(memory_space=pltpu.VMEM)
    outside = pl.BlockSpec(memory_space=pl.ANY)
    scalar = jax.ShapeDtypeStruct((1, 1), F32)
    shapes = [scalar, scalar, scalar, jax.ShapeDtypeStruct(args[4].shape, F32), *same, *same, *same, *copies]
    return pl.pallas_call(
        functools.partial(update_kernel, z),
        out_shape=tuple(shapes),
        in_specs=[inside] * 4 + [outside] + [inside] * (len(args) - 5),
        out_specs=tuple([inside] * 3 + [outside] + [inside] * (len(shapes) - 4)),
        scratch_shapes=[pltpu.VMEM(args[4].shape, F32), pltpu.SemaphoreType.DMA((2,))],
        compiler_params=pltpu.CompilerParams(vmem_limit_bytes=62 * 1024 * 1024),
        name="update",
    )(*args)


def solution(mesh):
    def local(
        features, hub_features, low_lists, low_masks, high_lists, high_masks, hub_lists, hub_masks, send_rows,
        labels, train_mask, stale_rows, weight_one, weight_two, weight_three, biases,
        mean_one, mean_two, mean_three, mean_biases, square_one, square_two, square_three, square_biases,
    ):
        z = Sizes(mesh, features, low_lists, high_lists, hub_lists, send_rows, weight_one, weight_three)
        three_t = weight_three.T
        two, upper, lower, renewed, misc = train(
            z, features.T, hub_features.T, low_lists.T, low_masks.T, high_lists.T, high_masks.T,
            hub_lists[0].T, hub_masks[0].T, send_rows[0],
            labels.reshape(-1, LANES), train_mask.reshape(-1, LANES), stale_rows,
            weight_one, weight_two, three_t, biases,
        )
        norm, loss, count, renewed, o1, o2, o3, ob, n1, n2, n3, nb, s1, s2, s3, sb, c1, c2, c3, cb = update(
            z, two, upper, lower, misc, renewed, weight_one, weight_two, three_t, biases,
            mean_one, mean_two, mean_three.T, mean_biases, square_one, square_two, square_three.T, square_biases,
        )
        return (
            norm[0, 0], loss[0, 0], count[0, 0],
            o1, o2, o3.T, ob, n1, n2, n3.T, nb, s1, s2, s3.T, sb, c1, c2, c3.T, cb, renewed,
        )

    spread = ("dom", "sub")
    rows, all_same, cube = P(spread, None), P(), P(spread, None, None)
    stale = P(None, spread, None)
    in_specs = (
        rows, all_same, rows, rows, rows, rows, cube, cube, cube, P(spread), P(spread), stale, *[all_same] * 12
    )
    out_specs = (*[all_same] * 19, stale)
    return jax.shard_map(local, mesh=mesh, in_specs=in_specs, out_specs=out_specs, check_vma=False)
```

time: 292 us -> 210 us (0.72)
  Pallas kernels: 253 us -> 209 us
  local copies, waits for them, and re-layouts: 32.4 us -> 0 us
  other arithmetic: 5.14 us -> 0 us
    pallas_call x1, Pallas kernels: 245 us -> 198 us  [train(): pl.pallas_call(functools.partial(train_kernel, z), out_shape=(*[jax.Shape...]
    unnamed x24 -> x0, local copies, waits for them, and re-layouts: 24.8 us -> none
    pallas_call x4 -> x0, other arithmetic: 5.14 us -> none  [update(): pl.pallas_call(functools.partial(update_kernel, z), out_shape=tuple(shape...]
    reshape x4 -> x0, local copies, waits for them, and re-layouts: 4.47 us -> none  [the longest x3 3.87 us: local(): line = lambda v: v.reshape(1, -1)]
where the time goes in v2:
time: 210 us
  Pallas kernels  209 us (100%)
    pallas_call x1, Pallas kernels, train(): pl.pallas_call(functools.partial(train_kernel, z), out_shape=(*[jax.Shape...  198 us
    pallas_call x1, Pallas kernels, update(): pl.pallas_call(functools.partial(update_kernel, z), out_shape=tuple(shape...  10.4 us

profile of v2, /device:TPU:0, one launch (start us, length us, event | category | flops | bytes accessed | tf_op | source)
XLA Modules:
  0.0 209.7 jit_solution(15173528178295715381)
XLA Ops:
  0.7 198.4 %train.1 = (f32[1280,128]{1,0:T(8,128)}, f32[1280,128]{1,0:T(8,128)}, f32[1280,128]{1,0:T(8,128)}, f32[2,1024,256]{2,1,0:T(8,128)}, f32[8,128]{1,0:T(8,128)}) custom-call(f32[602,512]{1,0:T(8,128)} %bitcast.25, f32[602,256]{1,0:T(8,128)} %bitcast.26, s32[4,256]{1,0:T(4,128)} %bitcast.36, s32[4,256]{1,0:T(4,128)} %bitcast.37, s32[32,256]{1,0:T(8,128)} %bitcast.31, ...), custom_call_target="tpu_custom_call" | custom-call | tf_op jit(solution)/shard_map/train/pallas_call | solution.py:895
  199.1 10.4 %update.1 = (f32[1,1]{1,0:T(1,128)}, f32[1,1]{1,0:T(1,128)}, f32[1,1]{1,0:T(1,128)}, f32[2,1024,256]{2,1,0:T(8,128)}, f32[1204,256]{1,0:T(8,128)}, /*index=5*/f3...) custom-call(f32[1280,128]{1,0:T(8,128)} %get-tuple-element.45.two, ...), custom_call_target="tpu_custom_call" | custom-call | tf_op jit(solution)/shard_map/update/pallas_call | solution.py:984

commit v3 on v2

--- a/solution.py
+++ b/solution.py
@@ -86,6 +86,7 @@
         self.shift = self.fin % 8
         self.brows = up(self.fin + self.shift, 8)
         self.part = self.hubs // self.dom
+        self.count_rows = self.hubs // LANES
         self.packed = self.blk % 16 == 0
         self.cblk = self.blk // 2 if self.packed else self.blk
         unit = 8 * self.devices
@@ -94,9 +95,10 @@
         self.flat = (
             up(self.at_three + self.hid, unit),
             up(self.at_bias + 8, unit),
-            up(self.halves * self.brows, unit),
+            *[up(self.brows, unit)] * self.halves,
         )
-        self.levels = (2, self.dom // 2, self.sub)
+        three, four = (2, self.dom // 2, self.sub), (2, self.dom // 2, 2, self.sub // 2)
+        self.levels = (four, four, *[three] * self.halves)
 
 
 class HubSum:
@@ -159,7 +161,7 @@
 
     def end(self):
         self.dom_done(self.out, 2)
-        return self.out[...].reshape(self.z.hubs, self.out.shape[-1])
+        return self.out[:, 0 : self.z.part, :].reshape(self.z.hubs, self.out.shape[-1])
 
 
 class FlatSum:
@@ -167,7 +169,8 @@
         d, s = place
         self.remote, self.index = remote, index
         self.source, self.out = buffers[0], buffers[1]
-        self.landed, self.parts = buffers[2:5], (buffers[0], *buffers[5:7])
+        depth = len(z.levels[index])
+        self.landed, self.parts = buffers[2 : 2 + depth], (buffers[0], *buffers[2 + depth :])
         self.sent, self.got = sems
         pair = lax.rem(d, 2)
         chip = d // 2
@@ -176,6 +179,13 @@
             (z.dom // 2, chip, lambda j: (j * 2 + pair, s)),
             (z.sub, s, lambda j: (d, j)),
         )
+        if depth == 4:
+            near, far = lax.rem(s, 2), s // 2
+            self.levels = (
+                *self.levels[:2],
+                (2, near, lambda j: (d, far * 2 + j)),
+                (z.sub // 2, far, lambda j: (d, j * 2 + near)),
+            )
         self.first, offset, rows = [], 0, self.source.shape[0]
         for size, mine, _ in self.levels:
             rows = rows // size
@@ -226,23 +236,23 @@
         @pl.loop(1, size)
         def _(k):
             j = lax.rem(mine + k, size)
-            self.remote(held, held, *self.sems(3 + level), *peer(j)).start()
+            self.remote(held, held, *self.sems(4 + level), *peer(j)).start()
 
     def collect(self, level):
         size, mine, peer = self.levels[level]
         some = self.out.at[pl.ds(0, (size - 1) * self.first[level][1])]
-        copy = self.remote(some, some, *self.sems(3 + level), *peer(lax.rem(mine + 1, size)))
+        copy = self.remote(some, some, *self.sems(4 + level), *peer(lax.rem(mine + 1, size)))
         copy.wait_recv()
         copy.wait_send()
 
 
-HUB_SUMS = (1, 1, 1, 1, 1, 1, 2)
+HUB_SUMS = (1, 1, 1, 1, 1, 2)
 
 
 def train_kernel(
     z,
     feat, hubf, lowl, lowm, highl, highm, hubl, hubm, send, lab, tmask, stale_hbm, w1, w2, w3, bias,
-    two_hbm, upper_hbm, lower_hbm, fresh_hbm, misc,
+    two_hbm, upper_hbm, lower_hbm, tail_hbm, fresh_hbm, misc,
     ab, abt, sel, selt, colb, keyt, keys, xh, xl, xth, xtl, w1h, w1l, w2h, w2l, w3t, w3h, w3l,
     tb, tc, inv, q, magg, h1h, h1l, m1h, m1l, h2h, h2l, dg0, dg1, dph, dpl, dmh, dml, eb, gown, gthree, stale,
     zst, pself, labc, trainw, brow,
@@ -289,8 +299,12 @@
     sums = [
         HubSum(z, place, remote, hub_refs[4 * i : 4 * i + 4], (hsem_s, hsem_r), i) for i in range(len(HUB_SUMS))
     ]
-    grads = [FlatSum(z, place, remote, flat_refs[7 * i : 7 * i + 7], (gsem_s, gsem_r), i) for i in range(3)]
-    two, upper, lower = grads
+    grads, start = [], 0
+    for i in range(len(z.flat)):
+        refs = flat_refs[start : start + 1 + 2 * len(z.levels[i])]
+        grads.append(FlatSum(z, place, remote, refs, (gsem_s, gsem_r), i))
+        start += len(refs)
+    two, upper, *lowers = grads
 
     def part_of(portion):
         return 1 + (z.devices - 1) * portion // 8
@@ -327,6 +341,55 @@
         return product[:, :LANES] + product[:, LANES:]
 
     per_tile = 256 // z.blk
+
+    def turn(source, target, r_count, c_count, c_start=0, step=128):
+        def body(r):
+            for c in range(c_start, c_count, step):
+                target[c : c + step, pl.ds(r, step)] = source[pl.ds(r, step), c : c + step].T
+
+        tiles(r_count, step, body)
+
+    pad0 = fin // 16 * 16
+    xth[pad0 : z.fpad, :] = jnp.zeros((z.fpad - pad0, z.rows), BF16)
+    xtl[pad0 : z.fpad, :] = jnp.zeros((z.fpad - pad0, z.rows), BF16)
+    w1h[pad0 : z.fpad, :] = jnp.zeros((z.fpad - pad0, 2 * hid), BF16)
+    w1l[pad0 : z.fpad, :] = jnp.zeros((z.fpad - pad0, 2 * hid), BF16)
+    put_pair(xth, xtl, slice(0, fin), own, feat[...])
+    turn(xth, xh, z.fpad, nd)
+    turn(xtl, xl, z.fpad, nd)
+    put_pair(w1h, w1l, slice(0, fin), low_rows, w1[fin : 2 * fin, :])
+
+    def project(rows, columns):
+        return three(dot, (xh[rows, :], xl[rows, :]), (w1h[:, columns], w1l[:, columns]))
+
+    def put_halves(rows, values):
+        for h in both:
+            put_split(tb.at[h], rows, values[:, lanes(h)])
+
+    tiles(nd, 256, lambda r: put_halves(pl.ds(r, 256), project(pl.ds(r, 256), low_rows)))
+
+    colb[0 : z.devices, 0 : z.blk] = send[...]
+    turned = colb[...].T
+
+    for tile in range(halo // 256):
+        first = tile * per_tile
+        column = jnp.concatenate([turned[0 : z.blk, p : p + 1] for p in range(first, first + per_tile)], axis=0)
+        hit = column == lax.broadcasted_iota(i32, (256, nd), 1)
+        sel[tile * 256 : tile * 256 + 256, :] = jnp.where(hit, 1.0, 0.0).astype(BF16)
+
+    def pick(source, target):
+        def body(r):
+            values = added(dot(sel[pl.ds(r, 256), :], source[own, :]))
+            target[pl.ds(r // z.blk, per_tile)] = values.reshape(per_tile, z.blk, LANES)
+
+        tiles(halo, 256, body)
+
+    pick(tb.at[0], send_a.at[0])
+    pl.semaphore_wait(barrier, z.devices - 1)
+    for h in both:
+        if h:
+            pick(tb.at[h], send_a.at[h])
+        exchange_start(send_a.at[h], recv_a.at[h], h)
 
     keyt[...] = jnp.full(keyt.shape, -1, i32)
     keyt[0 : z.k_low, 0 : z.low] = jnp.where(lowm[...] > 0, lowl[...], -1)
@@ -337,87 +400,28 @@
     counts = jnp.sum(jnp.where(keys[...] >= 0, 1.0, 0.0), axis=1, keepdims=True)
     inv[own, :] = 1.0 / jnp.maximum(counts[own, :], 1.0)
     train_local = jnp.sum(jnp.sum(tmask[...].astype(F32), axis=1, keepdims=True), axis=0, keepdims=True)
-    lane = lax.broadcasted_iota(i32, (hubs, LANES), 1)
-    sums[0].put(jnp.where(lane == 0, counts[hubq, :], jnp.where(lane == 1, train_local, 0.0)))
-
-    def turn(source, target, r_count, c_count, c_start=0, step=128):
-        def body(r):
-            for c in range(c_start, c_count, step):
-                target[c : c + step, pl.ds(r, step)] = source[pl.ds(r, step), c : c + step].T
-
-        tiles(r_count, step, body)
-
-    pad0 = fin // 16 * 16
-    xth[pad0 : z.fpad, :] = jnp.zeros((z.fpad - pad0, z.rows), BF16)
-    xtl[pad0 : z.fpad, :] = jnp.zeros((z.fpad - pad0, z.rows), BF16)
-    w1h[pad0 : z.fpad, :] = jnp.zeros((z.fpad - pad0, 2 * hid), BF16)
-    w1l[pad0 : z.fpad, :] = jnp.zeros((z.fpad - pad0, 2 * hid), BF16)
-    put_pair(xth, xtl, slice(0, fin), own, feat[...])
-    turn(xth, xh, z.fpad, nd)
-    turn(xtl, xl, z.fpad, nd)
-    pl.semaphore_wait(barrier, z.devices - 1)
-    sums[0].scatter()
-    put_pair(w1h, w1l, slice(0, fin), low_rows, w1[fin : 2 * fin, :])
-
-    def project(rows, columns):
-        return three(dot, (xh[rows, :], xl[rows, :]), (w1h[:, columns], w1l[:, columns]))
-
-    def put_halves(rows, values):
-        for h in both:
-            put_split(tb.at[h], rows, values[:, lanes(h)])
-
-    tiles(nd, 256, lambda r: put_halves(pl.ds(r, 256), project(pl.ds(r, 256), low_rows)))
-    sums[0].swap()
-
-    eye = lax.broadcasted_iota(i32, (z.blk, z.blk), 0) == lax.broadcasted_iota(i32, (z.blk, z.blk), 1)
-
-    @pl.loop(0, z.devices)
-    def _(p):
-        line = jnp.broadcast_to(send[pl.ds(p, 1), :], (z.blk, z.blk))
-        colb[pl.ds(pl.multiple_of(p * z.blk, z.blk), z.blk), :] = jnp.sum(
-            jnp.where(eye, line, 0), axis=1, keepdims=True
-        )
-
-    def sel_tile(r):
-        rows = pl.ds(r, 256)
-        sel[rows, :] = jnp.where(colb[rows, :] == lax.broadcasted_iota(i32, (256, nd), 1), 1.0, 0.0).astype(BF16)
-
-    tiles(halo, 256, sel_tile)
-
-    def pick(source, target):
-        def body(r):
-            values = added(dot(sel[pl.ds(r, 256), :], source[own, :]))
-            target[pl.ds(r // z.blk, per_tile)] = values.reshape(per_tile, z.blk, LANES)
-
-        tiles(halo, 256, body)
-
-    pick(tb.at[0], send_a.at[0])
-    sums[0].gather()
-    for h in both:
-        if h:
-            pick(tb.at[h], send_a.at[h])
-        exchange_start(send_a.at[h], recv_a.at[h], h)
+    used_slots = jnp.sum(jnp.where(keyt[0 : z.k_hub, hubq] >= 0, 1.0, 0.0), axis=0, keepdims=True)
+    extra = [used_slots[:, lanes(c)] for c in range(z.count_rows)] + [jnp.broadcast_to(train_local, (1, LANES))]
+    extra.append(jnp.zeros((8 - len(extra), LANES), F32))
+    extra = jnp.concatenate(extra, axis=0)
+    for block in range(z.dom):
+        sums[0].source[block, z.part : z.part + 8, :] = extra
 
     def build(first, count, slots):
-        width = z.table // 2
-
         def group(r):
             rows = pl.ds(first + r, 16)
-            key = keys[rows, :]
-            for half in range(2):
-                spot = lax.broadcasted_iota(i32, (16, width), 1) + half * width
-                total = jnp.zeros((16, width), F32)
-                for k in range(slots):
-                    total = total + jnp.where(key[:, k : k + 1] == spot, 1.0, 0.0)
-                ab[rows, half * width : (half + 1) * width] = total.astype(BF16)
+            key = keys[rows, :].astype(jnp.int16)
+            spot = lax.broadcasted_iota(i32, (16, z.table), 1).astype(jnp.int16)
+            one, none = jnp.ones((16, z.table), BF16), jnp.zeros((16, z.table), BF16)
+            total = none
+            for k in range(slots):
+                total = total + jnp.where(jnp.broadcast_to(key[:, k : k + 1], (16, z.table)) == spot, one, none)
+            ab[rows, :] = total
 
         tiles(count, 16, group)
 
     build(0, z.low, z.k_low)
     build(nd, hubs, z.k_hub)
-    hub_totals = sums[0].end()
-    inv[hubq, :] = 1.0 / hub_totals[:, 0:1]
-    misc[...] = hub_totals[0:8, :]
     build(z.low, z.high, z.k_high)
 
     put_pair(xth, xtl, slice(0, fin), hubq, hubf[...])
@@ -435,7 +439,7 @@
         rows = pl.ds(r, 256)
         q[rows, :] = project(rows, up_rows) + brow[0:1, :]
 
-    tiles(z.rows, 256, own_tile)
+    tiles(nd, 256, own_tile)
 
     def gather_local(h):
         def body(r):
@@ -444,12 +448,7 @@
 
         tiles(z.rows, 256, body)
 
-    for h in both:
-        gather_local(h)
-    put_pair(w2h, w2l, slice(0, 2 * hid), slice(0, hid), w2[...])
-    w3t[...] = jnp.zeros(w3t.shape, F32)
-    w3t[0 : z.cls, :] = w3[...]
-    put_pair(w3h, w3l, slice(0, 2 * hid), slice(0, LANES), w3t[...].T)
+    gather_local(0)
 
     def with_halo(rows, h):
         return magg[rows, lanes(h)] + added(dot(ab[rows, halos], tb[h, halos, :]))
@@ -465,32 +464,37 @@
 
         tiles(nd, 256, body)
 
-    def first_half():
-        exchange_wait(send_a.at[0], recv_a.at[0], 0)
-        put_split(tb.at[0], halos, recv_a[0].reshape(halo, LANES))
-        sums[1].put(with_halo(hubq, 0))
-        sums[1].scatter()
-        layer_one(0)
-        pick(tb.at[0], send_b.at[0])
-        exchange_start(send_b.at[0], recv_b.at[0], 2, 0, 4)
-
-    first_half()
+    exchange_wait(send_a.at[0], recv_a.at[0], 0)
+    put_split(tb.at[0], halos, recv_a[0].reshape(halo, LANES))
+    sums[0].source[:, 0 : z.part, :] = with_halo(hubq, 0).reshape(z.dom, z.part, LANES)
+    sums[0].scatter()
+    layer_one(0)
+    pick(tb.at[0], send_b.at[0])
+    exchange_start(send_b.at[0], recv_b.at[0], 2, 0, 4)
+    gather_local(1)
+    own_tile(nd)
+    turn(sel, selt, halo, nd)
     exchange_wait(send_a.at[1], recv_a.at[1], 1)
-    sums[1].swap()
     put_split(tb.at[1], halos, recv_a[1].reshape(halo, LANES))
-    sums[2].put(with_halo(hubq, 1))
-    sums[2].scatter()
+    sums[1].put(with_halo(hubq, 1))
+    sums[1].scatter()
     exchange_start(send_b.at[0], recv_b.at[0], 2, 4, 8)
     layer_one(1)
     pick(tb.at[1], send_b.at[1])
+    sums[0].swap()
+    sums[1].swap()
+    exchange_start(send_b.at[1], recv_b.at[1], 3, 0, 4)
+    put_pair(w2h, w2l, slice(0, 2 * hid), slice(0, hid), w2[...])
+    w3t[...] = jnp.zeros(w3t.shape, F32)
+    w3t[0 : z.cls, :] = w3[...]
+    put_pair(w3h, w3l, slice(0, 2 * hid), slice(0, LANES), w3t[...].T)
+    turn(ab, abt, z.rows, z.table)
+    sums[0].gather()
     sums[1].gather()
-    sums[2].swap()
-    exchange_start(send_b.at[1], recv_b.at[1], 3, 0, 4)
-    turn(ab, abt, z.rows, z.table)
-    sums[2].gather()
     exchange_start(send_b.at[1], recv_b.at[1], 3, 4, 8)
-
-    turn(sel, selt, halo, nd)
+    for grad in grads:
+        grad.source[...] = jnp.zeros(grad.source.shape, F32)
+
     stale_copy.wait()
     zst[...] = three(dot, split(KEEP * stale[1]), (w3h[low_rows, :], w3l[low_rows, :]))
     dg0[own, :] = gelu_slope(q[own, :])
@@ -500,8 +504,15 @@
         labc[lanes(block), :] = jnp.sum(jnp.where(diag, line, 0), axis=1, keepdims=True)
         line = jnp.broadcast_to(tmask[block : block + 1, :].astype(F32), (LANES, LANES))
         trainw[lanes(block), :] = jnp.sum(jnp.where(diag, line, 0.0), axis=1, keepdims=True)
+    first_hub = sums[0].end()
+    misc[...] = sums[0].out[0, z.part : z.part + 8, :]
+    colb[0:8, :] = misc[...].astype(i32)
+    turned_counts = colb[...].T
+    for c in range(z.count_rows):
+        inv[nd + c * LANES : nd + (c + 1) * LANES, :] = 1.0 / turned_counts[:, c : c + 1].astype(F32)
+    hub_ends = (first_hub, sums[1].end())
     for h in both:
-        pre = q[hubq, lanes(h)] + sums[1 + h].end() * inv[hubq, :]
+        pre = q[hubq, lanes(h)] + hub_ends[h] * inv[hubq, :]
         dg0[hubq, lanes(h)] = gelu_slope(pre)
         high, rest = put_pair(h1h, h1l, hubq, lanes(h), gelu(pre))
         tb[h, hubr, 0:LANES] = high
@@ -521,8 +532,8 @@
         renewed = KEEP * stale[0, :, lanes(h)] + (1.0 - KEEP) * recv_b[h].reshape(halo, LANES)
         stale[0, :, lanes(h)] = renewed
         put_split(tb.at[h], halos, renewed)
-        sums[3 + h].put(with_halo(hubq, h))
-        sums[3 + h].scatter()
+        sums[2 + h].put(with_halo(hubq, h))
+        sums[2 + h].scatter()
 
         def body(r):
             rows = pl.ds(r, 256)
@@ -531,9 +542,8 @@
         tiles(nd, 256, body)
 
     second(0)
-    sums[3].swap()
     second(1)
-    sums[3].gather()
+    sums[2].swap()
 
     def layer_two(r):
         rows = pl.ds(r, 256)
@@ -562,7 +572,8 @@
         send_c[pl.ds(r // z.blk, per_tile)] = pack(added(dot(sel[pl.ds(r, 256), :], tc[own, :])))
 
     tiles(halo, 256, pick_class)
-    sums[4].swap()
+    sums[3].swap()
+    sums[2].gather()
     exchange_start(send_c, recv_c, 4)
 
     def pick_wide(r):
@@ -570,41 +581,39 @@
         values = dot(chosen, h2l[own, :]) + dot(chosen, h2h[own, :])
         send_g[pl.ds(r // z.blk, per_tile)] = values.reshape(per_tile, z.blk, hid)
 
-    tiles(halo, 256, pick_wide)
-    sums[4].gather()
-    exchange_start(send_g, recv_g, 5, 0, 3)
 
     def own_three(r):
         rows = pl.ds(r, 256)
         pself[rows, :] = three(dot, (h2h[rows, :], h2l[rows, :]), (w3h[up_rows, :], w3l[up_rows, :])) + brow[2:3, 0:LANES]
 
     tiles(nd, 256, own_three)
+
+    def class_local(r):
+        rows = pl.ds(r, 256)
+        magg[rows, 0:LANES] = added(dot(ab[rows, own], tc[own, :]))
+
+    tiles(nd, 256, class_local)
+    sums[3].gather()
+    tiles(halo, 256, pick_wide)
+    exchange_start(send_g, recv_g, 5, 0, 2)
     dg1[own, :] = gelu_slope(q[own, :])
     for h in both:
-        put_pair(m1h, m1l, hubq, lanes(h), sums[3 + h].end() * inv[hubq, :])
+        put_pair(m1h, m1l, hubq, lanes(h), sums[2 + h].end() * inv[hubq, :])
     pre = q[hubq, :] + three(dot, (m1h[hubq, :], m1l[hubq, :]), (w2h[low_rows, :], w2l[low_rows, :]))
     high, rest = put_pair(h2h, h2l, hubq, slice(0, hid), gelu(pre))
     put_split(tc, hubr, three(dot, (high, rest), (w3h[low_rows, :], w3l[low_rows, :])))
     q[hubq, :] = pre
 
-    def class_local(r):
-        rows = pl.ds(r, 256)
-        magg[rows, 0:LANES] = added(dot(ab[rows, own], tc[own, :]) + dot(ab[rows, hubr], tc[hubr, :]))
-
-    tiles(nd, 256, class_local)
-
-    two.source[...] = jnp.zeros(two.source.shape, F32)
-    upper.source[...] = jnp.zeros(upper.source.shape, F32)
-    lower.source[...] = jnp.zeros(lower.source.shape, F32)
     exchange_wait(send_c, recv_c, 4)
+    exchange_start(send_g, recv_g, 5, 2, 3)
     put_split(tc, halos, zst[...] + (1.0 - KEEP) * unpack(recv_c[...]))
     used = lax.broadcasted_iota(i32, (256, LANES), 1)
-    train_total = misc[0:1, 1:2]
+    train_total = misc[z.count_rows : z.count_rows + 1, 0:1]
     at_bias = z.at_bias
 
     def head(r):
         rows = pl.ds(r, 256)
-        logits = pself[rows, :] + (magg[rows, 0:LANES] + added(dot(ab[rows, halos], tc[halos, :]))) * inv[rows, :]
+        logits = pself[rows, :] + (magg[rows, 0:LANES] + added(dot(ab[rows, halo0:], tc[halo0:, :]))) * inv[rows, :]
         valid = used < z.cls
         top = jnp.max(jnp.where(valid, logits, -1e30), axis=1, keepdims=True)
         shifted = logits - top
@@ -624,8 +633,8 @@
 
     tiles(nd, 256, head)
 
-    sums[5].put(added(dot(abt[hubr, own], eb[0, own, :])))
-    sums[5].scatter()
+    sums[4].put(added(dot(abt[hubr, own], eb[0, own, :])))
+    sums[4].scatter()
 
     def back_class(r):
         values = added(dot(abt[pl.ds(halo0 + r, 256), own], eb[0, own, :]))
@@ -633,14 +642,14 @@
         send_d[pl.ds(r // z.blk, per_tile)] = pack((1.0 - KEEP) * values)
 
     tiles(halo, 256, back_class)
-    sums[5].swap()
+    sums[4].swap()
     exchange_start(send_d, recv_d, 6)
     gown[own, 0:LANES] = added(dot(abt[own, own], eb[0, own, :]))
 
     gthree[:, 0:LANES] = three(dot_tn, split(KEEP * stale[1]), (tc[halos, 0:LANES], tc[halos, LANES : 2 * LANES]))
-    sums[5].gather()
-    exchange_start(send_g, recv_g, 5, 3, 6)
-    hub_class = split(sums[5].source[...].reshape(hubs, LANES))
+    sums[4].gather()
+    exchange_start(send_g, recv_g, 5, 3, 5)
+    hub_class = split(sums[4].source[...].reshape(hubs, LANES))
     gthree[:, 0:LANES] = gthree[:, 0:LANES] + three(dot_tn, (h2h[hubq, :], h2l[hubq, :]), hub_class)
     gthree[:, LANES : 2 * LANES] = three(dot_tn, (h2h[own, :], h2l[own, :]), (dph[own, 0:LANES], dpl[own, 0:LANES]))
     dg1[hubq, :] = gelu_slope(q[hubq, :])
@@ -662,7 +671,7 @@
     def column_sums(columns):
         return jnp.sum(dmh[:, columns].astype(F32) + dml[:, columns].astype(F32), axis=0, keepdims=True)
 
-    node = three(dot_nt, split(sums[5].end()), (w3h[low_rows, :], w3l[low_rows, :])) * dg1[hubq, :]
+    node = three(dot_nt, split(sums[4].end()), (w3h[low_rows, :], w3l[low_rows, :])) * dg1[hubq, :]
     put_pair(dph, dpl, hubq, slice(0, hid), node)
     put_pair(dmh, dml, hubq, slice(0, hid), owned(node))
 
@@ -673,6 +682,7 @@
 
     spread(hubq)
     exchange_wait(send_d, recv_d, 6)
+    exchange_start(send_g, recv_g, 5, 5, 6)
     put_split(tc, halos, unpack(recv_d[...]))
 
     def back_two(r):
@@ -690,8 +700,8 @@
     tiles(nd, 256, back_two)
 
     for h in both:
-        sums[6].source[:, :, lanes(h)] = added(dot(abt[hubr, :], eb[h])).reshape(z.dom, z.part, LANES)
-    sums[6].scatter()
+        sums[5].source[:, :, lanes(h)] = added(dot(abt[hubr, :], eb[h])).reshape(z.dom, z.part, LANES)
+    sums[5].scatter()
 
     def send_halo(target, factor, h):
         def body(r):
@@ -702,11 +712,9 @@
 
     send_halo(send_e.at[0], 1.0 - KEEP, 0)
     exchange_start(send_e.at[0], recv_e.at[0], 7, 0, 4)
-    sums[6].swap()
+    send_halo(send_e.at[1], 1.0 - KEEP, 1)
+    sums[5].swap()
     exchange_start(send_e.at[0], recv_e.at[0], 7, 4, 8)
-    send_halo(send_e.at[1], 1.0 - KEEP, 1)
-    sums[6].gather()
-    exchange_start(send_e.at[1], recv_e.at[1], 8, 0, 4)
 
     def own_back(r):
         rows = pl.ds(r, 256)
@@ -731,14 +739,17 @@
         two.source[start + hid : start + 2 * hid, :] = three(dot_tn, (m1h[...], m1l[...]), pair)
         at = at_bias + z.halves + h
         upper.source[at : at + 1, :] = column_sums(lanes(h))
+    sums[5].gather()
     two.send(0)
-    exchange_start(send_e.at[1], recv_e.at[1], 8, 4, 8)
-
-    node = (sums[6].end() + q[hubq, :]) * dg0[hubq, :]
+    exchange_start(send_e.at[1], recv_e.at[1], 8, 0, 4)
+    node = (sums[5].end() + q[hubq, :]) * dg0[hubq, :]
     put_pair(dmh, dml, hubq, slice(0, hid), owned(node))
     node = node * inv[hubq, :]
     for h in both:
         put_split(eb.at[h], hubq, node[:, lanes(h)])
+    two.receive(0)
+    two.send(1)
+    exchange_start(send_e.at[1], recv_e.at[1], 8, 4, 8)
 
     def back_one(h):
         exchange_wait(send_e.at[h], recv_e.at[h], 7 + h)
@@ -754,21 +765,21 @@
         send_halo(send_f.at[h], 1.0, h)
 
     back_one(0)
-    exchange_start(send_f.at[0], recv_f.at[0], 9)
-    two.receive(0)
-    two.send(1)
-    back_one(1)
-    exchange_start(send_f.at[1], recv_f.at[1], 10, 0, 4)
+    exchange_start(send_f.at[0], recv_f.at[0], 9, 0, 4)
     two.receive(1)
     two.send(2)
+    exchange_start(send_f.at[0], recv_f.at[0], 9, 4, 8)
+    back_one(1)
+    two.receive(2)
+    two.send(3)
     for h in both:
         top = three(dot, (xth[...], xtl[...]), (dmh[:, lanes(h)], dml[:, lanes(h)]))
         upper.source[h * z.frows : (h + 1) * z.frows, :] = top[0 : z.frows, :]
         upper.source[at_bias + h : at_bias + h + 1, :] = column_sums(lanes(h))
     upper.send(0)
-    exchange_start(send_f.at[1], recv_f.at[1], 10, 4, 8)
-    two.receive(2)
-    two.spread(2)
+    two.receive(3)
+    two.spread(3)
+    exchange_start(send_f.at[1], recv_f.at[1], 10, 0, 4)
 
     def own_last(r):
         rows = pl.ds(r, 256)
@@ -780,8 +791,8 @@
         put_pair(dmh, dml, hubq, lanes(h), added(dot(abt[hubr, :], eb[h])))
     upper.receive(0)
     upper.send(1)
-    two.collect(2)
-    two.spread(1)
+    two.collect(3)
+    two.spread(2)
 
     def last(h):
         exchange_wait(send_f.at[h], recv_f.at[h], 9 + h)
@@ -793,50 +804,73 @@
 
         tiles(nd, 256, body)
         bottom = three(dot, (xth[...], xtl[...]), (dmh[:, lanes(h)], dml[:, lanes(h)]))
-        start = h * z.brows + z.shift
-        lower.source[start : start + fin, :] = bottom[0:fin, :]
+        lowers[h].source[z.shift : z.shift + fin, :] = bottom[0:fin, :]
 
     last(0)
+    low_first, low_second = lowers
+    low_first.send(0)
+    exchange_start(send_f.at[1], recv_f.at[1], 10, 4, 8)
+    upper.receive(1)
+    upper.send(2)
+    two.collect(2)
+    two.spread(1)
+    low_first.receive(0)
+    low_first.send(1)
+    last(1)
+    low_second.send(0)
+    upper.receive(2)
+    upper.send(3)
     two.collect(1)
     two.spread(0)
-    upper.receive(1)
-    upper.send(2)
-    last(1)
-    lower.send(0)
-    exchange_start(send_g, recv_g, 5, 6, 8)
-    upper.receive(2)
-    upper.spread(2)
+    low_first.receive(1)
+    low_first.send(2)
+    exchange_start(send_g, recv_g, 5, 6, 7)
+    upper.receive(3)
+    upper.spread(3)
+    low_second.receive(0)
+    low_second.send(1)
     two.collect(0)
     two_copy = pltpu.make_async_copy(two.out, two_hbm, lsem.at[1])
     two_copy.start()
-    lower.receive(0)
-    lower.send(1)
+    upper.collect(3)
+    upper.spread(2)
+    low_first.receive(2)
+    low_first.spread(2)
+    exchange_start(send_g, recv_g, 5, 7, 8)
+    low_second.receive(1)
+    low_second.send(2)
+    low_first.collect(2)
+    low_first.spread(1)
     upper.collect(2)
     upper.spread(1)
-    lower.receive(1)
-    lower.send(2)
-    upper.collect(1)
-    upper.spread(0)
-    lower.receive(2)
-    lower.spread(2)
+    low_second.receive(2)
+    low_second.spread(2)
     exchange_wait(send_g, recv_g, 5)
     stale[1] = KEEP * stale[1] + (1.0 - KEEP) * recv_g[...].reshape(halo, hid)
     fresh_copy = pltpu.make_async_copy(stale, fresh_hbm, lsem.at[2])
     fresh_copy.start()
-    lower.collect(2)
-    lower.spread(1)
+    low_first.collect(1)
+    low_first.spread(0)
+    low_second.collect(2)
+    low_second.spread(1)
+    upper.collect(1)
+    upper.spread(0)
+    low_first.collect(0)
+    lower_copy = pltpu.make_async_copy(low_first.out, lower_hbm, lsem.at[4])
+    lower_copy.start()
     upper.collect(0)
     upper_copy = pltpu.make_async_copy(upper.out, upper_hbm, lsem.at[3])
     upper_copy.start()
-    lower.collect(1)
-    lower.spread(0)
-    lower.collect(0)
-    lower_copy = pltpu.make_async_copy(lower.out, lower_hbm, lsem.at[4])
-    lower_copy.start()
+    low_second.collect(1)
+    low_second.spread(0)
+    low_second.collect(0)
+    tail_copy = pltpu.make_async_copy(low_second.out, tail_hbm, lsem.at[5])
+    tail_copy.start()
     two_copy.wait()
     fresh_copy.wait()
     upper_copy.wait()
     lower_copy.wait()
+    tail_copy.wait()
 
 
 def train(z, *args):
@@ -847,28 +881,23 @@
     bulk = (z.devices, z.blk, hid)
     thin = (z.devices, z.cblk, LANES)
 
-    def hub_buffers(count):
+    def hub_buffers(count, more):
         width = count * LANES
-        return [
-            vmem((z.dom, z.part, width), f),
-            vmem((z.dom, z.part, width), f),
-            vmem((z.sub, z.part, width), f),
-            vmem((z.dom, z.part, width), f),
-        ]
-
-    def flat_buffers(total):
+        return [vmem((size, z.part + more, width), f) for size in (z.dom, z.dom, z.sub, z.dom)]
+
+    def flat_buffers(total, levels):
         landed, parts, rest = [], [], total
-        for size in z.levels:
+        for size in levels:
             rest = rest // size
             landed.append(vmem((size, rest, LANES), f))
             parts.append(vmem((rest, LANES), f))
-        return [vmem((total, LANES), f), vmem((total, LANES), f), *landed, *parts[:2]]
+        return [vmem((total, LANES), f), vmem((total, LANES), f), *landed, *parts[:-1]]
 
     def pairs(count, *shape):
         return [vmem(shape, b) for _ in range(2 * count)]
 
     scratch = [
-        vmem((rows, tab), b), vmem((tab, rows), b), vmem((halo, n), b), vmem((n, halo), b), vmem((halo, 1), i),
+        vmem((rows, tab), b), vmem((tab, rows), b), vmem((halo, n), b), vmem((n, halo), b), vmem((LANES, LANES), i),
         vmem((LANES, rows), i), vmem((rows, LANES), i),
         *pairs(1, rows, z.fpad), *pairs(1, z.fpad, rows), *pairs(1, z.fpad, 2 * hid), *pairs(1, 2 * hid, hid),
         vmem((LANES, 2 * hid), f), *pairs(1, 2 * hid, LANES),
@@ -882,13 +911,13 @@
         vmem((halo, LANES), f), vmem((n, LANES), f), vmem((n, 1), i), vmem((n, 1), f), vmem((8, hid), f),
         *[vmem(shape, f) for shape in (wide, wide, wide, wide, thin, thin, thin, thin, wide, wide, bulk, bulk)],
     ]
-    for count in HUB_SUMS:
-        scratch += hub_buffers(count)
-    for total in z.flat:
-        scratch += flat_buffers(total)
+    for index, count in enumerate(HUB_SUMS):
+        scratch += hub_buffers(count, 0 if index else 8)
+    for total, levels in zip(z.flat, z.levels):
+        scratch += flat_buffers(total, levels)
     dma = pltpu.SemaphoreType.DMA
     scratch += [
-        dma((11,)), dma((11,)), dma((len(HUB_SUMS), 3)), dma((len(HUB_SUMS), 3)), dma((3, 6)), dma((3, 6)), dma((5,))
+        dma((11,)), dma((11,)), dma((len(HUB_SUMS), 3)), dma((len(HUB_SUMS), 3)), dma((len(z.flat), 8)), dma((len(z.flat), 8)), dma((4 + z.halves,))
     ]
     inside = pl.BlockSpec(memory_space=pltpu.VMEM)
     outside = pl.BlockSpec(memory_space=pl.ANY)
@@ -900,7 +929,7 @@
             jax.ShapeDtypeStruct((8, LANES), f),
         ),
         in_specs=[inside] * 11 + [outside] + [inside] * 4,
-        out_specs=(outside, outside, outside, outside, inside),
+        out_specs=(outside, outside, outside, outside, outside, inside),
         scratch_shapes=scratch,
         compiler_params=pltpu.CompilerParams(
             collective_id=0, has_side_effects=True, vmem_limit_bytes=62 * 1024 * 1024
@@ -909,84 +938,134 @@
     )(*args)
 
 
-def update_kernel(z, two, upper, lower, misc, fresh, w1, w2, w3, bs, m1, m2, m3, mb, v1, v2, v3, vb,
-                  o_norm, o_loss, o_count, o_fresh, o1, o2, o3, ob, n1, n2, n3, nb, s1, s2, s3, sb, c1, c2, c3, cb,
-                  held, sem):
-    taken = pltpu.make_async_copy(fresh, held, sem.at[0])
-    taken.start()
+def update_kernel(
+    z,
+    two_hbm, upper_hbm, low_a_hbm, low_b_hbm, fresh_hbm, w1_hbm, m1_hbm, v1_hbm, w2_hbm, m2_hbm, v2_hbm,
+    misc, w3, m3, v3, bs, mb, vb,
+    o1, n1, s1, c1, o2, n2, s2, c2, o_fresh,
+    o_norm, o_loss, o_count, o3, n3, s3, c3, ob, nb, sb, cb,
+    two, upper, low_a, low_b, held, w1, m1, v1, w2, m2, v2, d1, d2, in_sem, out_sem,
+):
+    inward = [
+        pltpu.make_async_copy(src, dst, in_sem.at[i])
+        for i, (src, dst) in enumerate(
+            (
+                (two_hbm, two), (upper_hbm, upper), (low_a_hbm, low_a), (low_b_hbm, low_b),
+                (w1_hbm, w1), (m1_hbm, m1), (v1_hbm, v1), (w2_hbm, w2), (m2_hbm, m2), (v2_hbm, v2), (fresh_hbm, held),
+            )
+        )
+    ]
+    for copy in inward:
+        copy.start()
+    outward = []
+
+    def leave(src, dst, rows=None):
+        if rows is not None:
+            src, dst = src.at[rows], dst.at[rows]
+        outward.append(pltpu.make_async_copy(src, dst, out_sem.at[len(outward)]))
+        outward[-1].start()
 
     def squares(values):
         return jnp.sum(jnp.sum(values * values, axis=0, keepdims=True), axis=1, keepdims=True)
 
     at_loss = z.at_bias + 2 * z.halves + 1
-    norm = jnp.sqrt(squares(two[...]) + squares(upper[0:at_loss, :]) + squares(lower[...]))
+    for copy in inward[:4]:
+        copy.wait()
+    norm = jnp.sqrt(
+        squares(two[...]) + squares(upper[0:at_loss, :]) + squares(low_a[...]) + squares(low_b[...])
+    )
     o_norm[...] = norm
     o_loss[...] = upper[at_loss : at_loss + 1, 0:1]
-    o_count[...] = misc[0:1, 1:2]
+    o_count[...] = misc[z.count_rows : z.count_rows + 1, 0:1]
     factor = jnp.minimum(1.0, CLIP / (norm + 1e-06))
 
-    def renew(rows, lanes, grad, w, m, v, ow, om, ov, oc=None):
+    def step(grad, old, first, second):
         clipped = grad * factor
-        moment = 0.5 * m[rows, lanes] + 0.5 * clipped
-        second = 0.5 * v[rows, lanes] + 0.5 * clipped * clipped
-        old = w[rows, lanes]
-        om[rows, lanes] = moment
-        ov[rows, lanes] = second
-        fresh_weight = old - RATE * ((moment / CORRECT) / (jnp.sqrt(second / CORRECT) + EPSILON) + DECAY * old)
-        ow[rows, lanes] = fresh_weight
-        if oc is not None:
-            oc[rows, lanes] = fresh_weight.astype(BF16)
-
-    taken.wait()
-    moved = pltpu.make_async_copy(held, o_fresh, sem.at[1])
-    moved.start()
+        moment = 0.5 * first + 0.5 * clipped
+        squared = 0.5 * second + 0.5 * clipped * clipped
+        fresh = old - RATE * ((moment / CORRECT) / (jnp.sqrt(squared / CORRECT) + EPSILON) + DECAY * old)
+        return fresh, moment, squared
+
+    def renew(rows, lanes, grad, w, m, v):
+        w[rows, lanes], m[rows, lanes], v[rows, lanes] = step(grad, w[rows, lanes], m[rows, lanes], v[rows, lanes])
+
+    def lane_half(half):
+        return slice(half * LANES, (half + 1) * LANES)
+
     low = z.fin - z.shift
+    lows = (low_a, low_b)
+    for copy in inward[4:7]:
+        copy.wait()
     for half in range(z.halves):
-        lanes = slice(half * LANES, (half + 1) * LANES)
-        u0, l0 = half * z.frows, half * z.brows
-        one = (w1, m1, v1, o1, n1, s1)
-        renew(slice(0, low), lanes, upper[u0 : u0 + low, :], *one)
+        u0 = half * z.frows
+        renew(slice(0, low), lane_half(half), upper[u0 : u0 + low, :], w1, m1, v1)
+    for src, dst in ((w1, o1), (m1, n1), (v1, s1)):
+        leave(src, dst, pl.ds(0, low))
+    for half in range(z.halves):
+        u0, lower, lanes = half * z.frows, lows[half], lane_half(half)
         if z.shift:
-            renew(slice(low, low + 8), lanes, upper[u0 + low : u0 + low + 8, :] + lower[l0 : l0 + 8, :], *one)
-            renew(slice(low + 8, 2 * z.fin), lanes, lower[l0 + 8 : l0 + z.fin + z.shift, :], *one)
+            renew(slice(low, low + 8), lanes, upper[u0 + low : u0 + low + 8, :] + lower[0:8, :], w1, m1, v1)
+            renew(slice(low + 8, 2 * z.fin), lanes, lower[8 : z.fin + z.shift, :], w1, m1, v1)
         else:
-            renew(slice(low, 2 * z.fin), lanes, lower[l0 : l0 + z.fin, :], *one)
+            renew(slice(low, 2 * z.fin), lanes, lower[0 : z.fin, :], w1, m1, v1)
+    for src, dst in ((w1, o1), (m1, n1), (v1, s1)):
+        leave(src, dst, pl.ds(low, 2 * z.fin - low))
+    d1[...] = w1[...].astype(BF16)
+    leave(d1, c1)
+    for copy in inward[7:10]:
+        copy.wait()
+    for half in range(z.halves):
         start = half * 2 * z.hid
-        renew(slice(0, 2 * z.hid), lanes, two[start : start + 2 * z.hid, :], w2, m2, v2, o2, n2, s2, c2)
+        renew(slice(0, 2 * z.hid), lane_half(half), two[start : start + 2 * z.hid, :], w2, m2, v2)
+    for src, dst in ((w2, o2), (m2, n2), (v2, s2)):
+        leave(src, dst)
+    d2[...] = w2[...].astype(BF16)
+    leave(d2, c2)
+    inward[10].wait()
+    leave(held, o_fresh)
     packed = two[z.at_three : z.at_three + z.hid, :].T
     for half in range(2):
         grad = packed[half * (LANES // 2) : half * (LANES // 2) + z.cls, :]
-        renew(slice(0, z.cls), slice(half * z.hid, (half + 1) * z.hid), grad, w3, m3, v3, o3, n3, s3, c3)
-    c1[...] = o1[...].astype(BF16)
+        part = slice(half * z.hid, (half + 1) * z.hid)
+        fresh, moment, squared = step(grad, w3[:, part], m3[:, part], v3[:, part])
+        o3[:, part] = fresh
+        n3[:, part] = moment
+        s3[:, part] = squared
+        c3[:, part] = fresh.astype(BF16)
     size = bs.shape[0]
     line = jnp.concatenate([upper[z.at_bias + k : z.at_bias + k + 1, :] for k in range(2 * z.halves + 1)], axis=1)
-    clipped = line[:, 0:size] * factor
     flat = lambda ref: ref[...].reshape(1, size)
-    moment = 0.5 * flat(mb) + 0.5 * clipped
-    second = 0.5 * flat(vb) + 0.5 * clipped * clipped
-    old = flat(bs)
-    fresh_bias = old - RATE * ((moment / CORRECT) / (jnp.sqrt(second / CORRECT) + EPSILON) + DECAY * old)
-    ob[...] = fresh_bias.reshape(size)
+    fresh, moment, squared = step(line[:, 0:size], flat(bs), flat(mb), flat(vb))
+    ob[...] = fresh.reshape(size)
     nb[...] = moment.reshape(size)
-    sb[...] = second.reshape(size)
+    sb[...] = squared.reshape(size)
     cb[...] = ob[...].astype(BF16)
-    moved.wait()
+    for copy in outward:
+        copy.wait()
 
 
 def update(z, *args):
-    weights = args[5:9]
-    same = [jax.ShapeDtypeStruct(w.shape, F32) for w in weights]
-    copies = [jax.ShapeDtypeStruct(w.shape, BF16) for w in weights]
     inside = pl.BlockSpec(memory_space=pltpu.VMEM)
     outside = pl.BlockSpec(memory_space=pl.ANY)
-    scalar = jax.ShapeDtypeStruct((1, 1), F32)
-    shapes = [scalar, scalar, scalar, jax.ShapeDtypeStruct(args[4].shape, F32), *same, *same, *same, *copies]
+    shape = jax.ShapeDtypeStruct
+    one, two, three_t, line = args[5].shape, args[8].shape, args[12].shape, args[15].shape
+
+    def group(size):
+        return [shape(size, F32)] * 3 + [shape(size, BF16)]
+
+    shapes = [
+        *group(one), *group(two), shape(args[4].shape, F32), *[shape((1, 1), F32)] * 3, *group(three_t), *group(line)
+    ]
     return pl.pallas_call(
         functools.partial(update_kernel, z),
         out_shape=tuple(shapes),
-        in_specs=[inside] * 4 + [outside] + [inside] * (len(args) - 5),
-        out_specs=tuple([inside] * 3 + [outside] + [inside] * (len(shapes) - 4)),
-        scratch_shapes=[pltpu.VMEM(args[4].shape, F32), pltpu.SemaphoreType.DMA((2,))],
+        in_specs=[outside] * 11 + [inside] * 7,
+        out_specs=tuple([outside] * 9 + [inside] * 11),
+        scratch_shapes=[
+            *[pltpu.VMEM(a.shape, F32) for a in args[:11]],
+            pltpu.VMEM(one, BF16), pltpu.VMEM(two, BF16),
+            pltpu.SemaphoreType.DMA((11,)), pltpu.SemaphoreType.DMA((12,)),
+        ],
         compiler_params=pltpu.CompilerParams(vmem_limit_bytes=62 * 1024 * 1024),
         name="update",
     )(*args)
@@ -1000,15 +1079,16 @@
     ):
         z = Sizes(mesh, features, low_lists, high_lists, hub_lists, send_rows, weight_one, weight_three)
         three_t = weight_three.T
-        two, upper, lower, renewed, misc = train(
+        two, upper, low_first, low_second, renewed, misc = train(
             z, features.T, hub_features.T, low_lists.T, low_masks.T, high_lists.T, high_masks.T,
             hub_lists[0].T, hub_masks[0].T, send_rows[0],
             labels.reshape(-1, LANES), train_mask.reshape(-1, LANES), stale_rows,
             weight_one, weight_two, three_t, biases,
         )
-        norm, loss, count, renewed, o1, o2, o3, ob, n1, n2, n3, nb, s1, s2, s3, sb, c1, c2, c3, cb = update(
-            z, two, upper, lower, misc, renewed, weight_one, weight_two, three_t, biases,
-            mean_one, mean_two, mean_three.T, mean_biases, square_one, square_two, square_three.T, square_biases,
+        o1, n1, s1, c1, o2, n2, s2, c2, renewed, norm, loss, count, o3, n3, s3, c3, ob, nb, sb, cb = update(
+            z, two, upper, low_first, low_second, renewed, weight_one, mean_one, square_one,
+            weight_two, mean_two, square_two, misc, three_t, mean_three.T, square_three.T,
+            biases, mean_biases, square_biases,
         )
         return (
             norm[0, 0], loss[0, 0], count[0, 0],

time: 210 us -> 195 us (0.929)
  Pallas kernels: 209 us -> 194 us
    pallas_call x1, Pallas kernels: 198 us -> 185 us  [train(): pl.pallas_call(functools.partial(train_kernel, z), out_shape=(*[jax.Shape...]
where the time goes in v3:
time: 195 us
  Pallas kernels  194 us (99%)
    pallas_call x1, Pallas kernels, train(): pl.pallas_call(functools.partial(train_kernel, z), out_shape=(*[jax.Shape...  185 us
    pallas_call x1, Pallas kernels, update(): pl.pallas_call(functools.partial(update_kernel, z), out_shape=tuple(shape...  9.21 us

profile of v3, /device:TPU:0, one launch (start us, length us, event | category | flops | bytes accessed | tf_op | source)
XLA Modules:
  0.0 194.7 jit_solution(4333817501168560087)
XLA Ops:
  0.7 184.6 %train.1 = (f32[1280,128]{1,0:T(8,128)}, f32[1280,128]{1,0:T(8,128)}, f32[768,128]{1,0:T(8,128)}, f32[768,128]{1,0:T(8,128)}, f32[2,1024,256]{2,1,0:T(8,128)}, /*index=5*/f32[8,128]{1,0:T(8,128)}) custom-call(f32[602,512]{1,0:T(8,128)} %bitcast.25, f32[602,256]{1,0:T(8,128)} %bitcast.26, s32[4,256]{1,0:T(4,128)} %bitcast.36, s32[4,256]{1,0:T(4,128)} %bitcast.37, ...), custom_call_target="tpu_custom_call" | custom-call | tf_op jit(solution)/shard_map/train/pallas_call | solution.py:924
  185.3 9.2 %update.1 = (f32[1204,256]{1,0:T(8,128)}, f32[1204,256]{1,0:T(8,128)}, f32[1204,256]{1,0:T(8,128)}, bf16[1204,256]{1,0:T(8,128)(2,1)}, f32[512,256]{1,0:T(8,128)...) custom-call(f32[1280,128]{1,0:T(8,128)} %get-tuple-element.46.two_hb, ...), custom_call_target="tpu_custom_call" | custom-call | tf_op jit(solution)/shard_map/update/pallas_call | solution.py:1059

commit v4 on v3

--- a/solution.py
+++ b/solution.py
@@ -87,6 +87,8 @@
         self.brows = up(self.fin + self.shift, 8)
         self.part = self.hubs // self.dom
         self.count_rows = self.hubs // LANES
+        self.paired = self.part % 16 == 0
+        self.class_part = self.part // 2 if self.paired else self.part
         self.packed = self.blk % 16 == 0
         self.cblk = self.blk // 2 if self.packed else self.blk
         unit = 8 * self.devices
@@ -159,8 +161,11 @@
         self.out[d] = total
         self.over_dom(lambda pd: (self.out.at[d], self.out.at[d]), 2)
 
+    def finish(self):
+        self.dom_done(self.out, 2)
+
     def end(self):
-        self.dom_done(self.out, 2)
+        self.finish()
         return self.out[:, 0 : self.z.part, :].reshape(self.z.hubs, self.out.shape[-1])
 
 
@@ -312,8 +317,9 @@
     def exchange_start(src, dst, i, first=0, last=8):
         @pl.loop(part_of(first), part_of(last))
         def _(k):
-            pd = lax.rem(d + k // z.sub, z.dom)
-            ps = lax.rem(s + k % z.sub, z.sub)
+            mixed = lax.rem(k * 5, z.devices)
+            pd = lax.rem(d + mixed // z.sub, z.dom)
+            ps = lax.rem(s + mixed % z.sub, z.sub)
             remote(src.at[pd * z.sub + ps], dst.at[me], xs.at[i], xr.at[i], pd, ps).start()
 
         if first == 0:
@@ -595,7 +601,7 @@
     tiles(nd, 256, class_local)
     sums[3].gather()
     tiles(halo, 256, pick_wide)
-    exchange_start(send_g, recv_g, 5, 0, 2)
+    exchange_start(send_g, recv_g, 5, 0, 3)
     dg1[own, :] = gelu_slope(q[own, :])
     for h in both:
         put_pair(m1h, m1l, hubq, lanes(h), sums[2 + h].end() * inv[hubq, :])
@@ -605,7 +611,6 @@
     q[hubq, :] = pre
 
     exchange_wait(send_c, recv_c, 4)
-    exchange_start(send_g, recv_g, 5, 2, 3)
     put_split(tc, halos, zst[...] + (1.0 - KEEP) * unpack(recv_c[...]))
     used = lax.broadcasted_iota(i32, (256, LANES), 1)
     train_total = misc[z.count_rows : z.count_rows + 1, 0:1]
@@ -633,7 +638,21 @@
 
     tiles(nd, 256, head)
 
-    sums[4].put(added(dot(abt[hubr, own], eb[0, own, :])))
+
+    def pack_hubs(values):
+        blocks = values.reshape(z.dom, z.part, LANES)
+        if z.paired:
+            return blocks[:, : z.class_part] + pltpu.roll(blocks[:, z.class_part :], LANES // 2, 2)
+        return blocks
+
+    def unpack_hubs(blocks):
+        if z.paired:
+            first = jnp.where(class_lane, blocks, 0.0)
+            second = jnp.where(class_lane, pltpu.roll(blocks, LANES // 2, 2), 0.0)
+            blocks = jnp.concatenate([first, second], axis=1)
+        return blocks.reshape(hubs, LANES)
+
+    sums[4].put(pack_hubs(added(dot(abt[hubr, own], eb[0, own, :]))))
     sums[4].scatter()
 
     def back_class(r):
@@ -648,8 +667,8 @@
 
     gthree[:, 0:LANES] = three(dot_tn, split(KEEP * stale[1]), (tc[halos, 0:LANES], tc[halos, LANES : 2 * LANES]))
     sums[4].gather()
-    exchange_start(send_g, recv_g, 5, 3, 5)
-    hub_class = split(sums[4].source[...].reshape(hubs, LANES))
+    exchange_start(send_g, recv_g, 5, 3, 6)
+    hub_class = split(unpack_hubs(sums[4].source[...]))
     gthree[:, 0:LANES] = gthree[:, 0:LANES] + three(dot_tn, (h2h[hubq, :], h2l[hubq, :]), hub_class)
     gthree[:, LANES : 2 * LANES] = three(dot_tn, (h2h[own, :], h2l[own, :]), (dph[own, 0:LANES], dpl[own, 0:LANES]))
     dg1[hubq, :] = gelu_slope(q[hubq, :])
@@ -671,7 +690,8 @@
     def column_sums(columns):
         return jnp.sum(dmh[:, columns].astype(F32) + dml[:, columns].astype(F32), axis=0, keepdims=True)
 
-    node = three(dot_nt, split(sums[4].end()), (w3h[low_rows, :], w3l[low_rows, :])) * dg1[hubq, :]
+    sums[4].finish()
+    node = three(dot_nt, split(unpack_hubs(sums[4].out[...])), (w3h[low_rows, :], w3l[low_rows, :])) * dg1[hubq, :]
     put_pair(dph, dpl, hubq, slice(0, hid), node)
     put_pair(dmh, dml, hubq, slice(0, hid), owned(node))
 
@@ -682,7 +702,6 @@
 
     spread(hubq)
     exchange_wait(send_d, recv_d, 6)
-    exchange_start(send_g, recv_g, 5, 5, 6)
     put_split(tc, halos, unpack(recv_d[...]))
 
     def back_two(r):
@@ -740,15 +759,13 @@
         at = at_bias + z.halves + h
         upper.source[at : at + 1, :] = column_sums(lanes(h))
     sums[5].gather()
-    two.send(0)
     exchange_start(send_e.at[1], recv_e.at[1], 8, 0, 4)
     node = (sums[5].end() + q[hubq, :]) * dg0[hubq, :]
     put_pair(dmh, dml, hubq, slice(0, hid), owned(node))
     node = node * inv[hubq, :]
     for h in both:
         put_split(eb.at[h], hubq, node[:, lanes(h)])
-    two.receive(0)
-    two.send(1)
+    two.send(0)
     exchange_start(send_e.at[1], recv_e.at[1], 8, 4, 8)
 
     def back_one(h):
@@ -766,19 +783,19 @@
 
     back_one(0)
     exchange_start(send_f.at[0], recv_f.at[0], 9, 0, 4)
+    two.receive(0)
+    two.send(1)
+    exchange_start(send_f.at[0], recv_f.at[0], 9, 4, 8)
+    back_one(1)
     two.receive(1)
     two.send(2)
-    exchange_start(send_f.at[0], recv_f.at[0], 9, 4, 8)
-    back_one(1)
-    two.receive(2)
-    two.send(3)
     for h in both:
         top = three(dot, (xth[...], xtl[...]), (dmh[:, lanes(h)], dml[:, lanes(h)]))
         upper.source[h * z.frows : (h + 1) * z.frows, :] = top[0 : z.frows, :]
         upper.source[at_bias + h : at_bias + h + 1, :] = column_sums(lanes(h))
     upper.send(0)
-    two.receive(3)
-    two.spread(3)
+    two.receive(2)
+    two.send(3)
     exchange_start(send_f.at[1], recv_f.at[1], 10, 0, 4)
 
     def own_last(r):
@@ -791,8 +808,8 @@
         put_pair(dmh, dml, hubq, lanes(h), added(dot(abt[hubr, :], eb[h])))
     upper.receive(0)
     upper.send(1)
-    two.collect(3)
-    two.spread(2)
+    two.receive(3)
+    two.spread(3)
 
     def last(h):
         exchange_wait(send_f.at[h], recv_f.at[h], 9 + h)
@@ -810,33 +827,32 @@
     low_first, low_second = lowers
     low_first.send(0)
     exchange_start(send_f.at[1], recv_f.at[1], 10, 4, 8)
+    exchange_start(send_g, recv_g, 5, 6, 8)
     upper.receive(1)
     upper.send(2)
-    two.collect(2)
-    two.spread(1)
+    two.collect(3)
+    two.spread(2)
     low_first.receive(0)
     low_first.send(1)
     last(1)
     low_second.send(0)
     upper.receive(2)
     upper.send(3)
-    two.collect(1)
-    two.spread(0)
+    two.collect(2)
+    two.spread(1)
     low_first.receive(1)
     low_first.send(2)
-    exchange_start(send_g, recv_g, 5, 6, 7)
     upper.receive(3)
     upper.spread(3)
     low_second.receive(0)
     low_second.send(1)
-    two.collect(0)
+    two.collect(1)
+    two.spread(0)
     two_copy = pltpu.make_async_copy(two.out, two_hbm, lsem.at[1])
-    two_copy.start()
     upper.collect(3)
     upper.spread(2)
     low_first.receive(2)
     low_first.spread(2)
-    exchange_start(send_g, recv_g, 5, 7, 8)
     low_second.receive(1)
     low_second.send(2)
     low_first.collect(2)
@@ -855,6 +871,8 @@
     low_second.spread(1)
     upper.collect(1)
     upper.spread(0)
+    two.collect(0)
+    two_copy.start()
     low_first.collect(0)
     lower_copy = pltpu.make_async_copy(low_first.out, lower_hbm, lsem.at[4])
     lower_copy.start()
@@ -912,7 +930,7 @@
         *[vmem(shape, f) for shape in (wide, wide, wide, wide, thin, thin, thin, thin, wide, wide, bulk, bulk)],
     ]
     for index, count in enumerate(HUB_SUMS):
-        scratch += hub_buffers(count, 0 if index else 8)
+        scratch += hub_buffers(count, {0: 8, 4: z.class_part - z.part}.get(index, 0))
     for total, levels in zip(z.flat, z.levels):
         scratch += flat_buffers(total, levels)
     dma = pltpu.SemaphoreType.DMA
@@ -983,7 +1001,8 @@
         clipped = grad * factor
         moment = 0.5 * first + 0.5 * clipped
         squared = 0.5 * second + 0.5 * clipped * clipped
-        fresh = old - RATE * ((moment / CORRECT) / (jnp.sqrt(squared / CORRECT) + EPSILON) + DECAY * old)
+        below = jnp.sqrt(squared * (1.0 / CORRECT)) + EPSILON
+        fresh = old * (1.0 - RATE * DECAY) - (moment * (RATE / CORRECT)) / below
         return fresh, moment, squared
 
     def renew(rows, lanes, grad, w, m, v):

time: 195 us -> 190 us (0.974)
  Pallas kernels: 194 us -> 189 us
    pallas_call x1, Pallas kernels: 185 us -> 180 us  [train(): pl.pallas_call(functools.partial(train_kernel, z), out_shape=(*[jax.Shape...]
where the time goes in v4:
time: 190 us
  Pallas kernels  189 us (99%)
    pallas_call x1, Pallas kernels, train(): pl.pallas_call(functools.partial(train_kernel, z), out_shape=(*[jax.Shape...  180 us
    pallas_call x1, Pallas kernels, update(): pl.pallas_call(functools.partial(update_kernel, z), out_shape=tuple(shape...  9.09 us

profile of v4, /device:TPU:0, one launch (start us, length us, event | category | flops | bytes accessed | tf_op | source)
XLA Modules:
  0.0 190.2 jit_solution(800222335228889558)
XLA Ops:
  0.7 180.2 %train.1 = (f32[1280,128]{1,0:T(8,128)}, f32[1280,128]{1,0:T(8,128)}, f32[768,128]{1,0:T(8,128)}, f32[768,128]{1,0:T(8,128)}, f32[2,1024,256]{2,1,0:T(8,128)}, /*index=5*/f32[8,128]{1,0:T(8,128)}) custom-call(f32[602,512]{1,0:T(8,128)} %bitcast.25, f32[602,256]{1,0:T(8,128)} %bitcast.26, s32[4,256]{1,0:T(4,128)} %bitcast.36, s32[4,256]{1,0:T(4,128)} %bitcast.37, ...), custom_call_target="tpu_custom_call" | custom-call | tf_op jit(solution)/shard_map/train/pallas_call | solution.py:942
  180.9 9.1 %update.1 = (f32[1204,256]{1,0:T(8,128)}, f32[1204,256]{1,0:T(8,128)}, f32[1204,256]{1,0:T(8,128)}, bf16[1204,256]{1,0:T(8,128)(2,1)}, f32[512,256]{1,0:T(8,128)...) custom-call(f32[1280,128]{1,0:T(8,128)} %get-tuple-element.46.two_hb, ...), custom_call_target="tpu_custom_call" | custom-call | tf_op jit(solution)/shard_map/update/pallas_call | solution.py:1078

commit v5 on v4

--- a/solution.py
+++ b/solution.py
@@ -22,6 +22,7 @@
 GELU_A = 0.7978845608
 GELU_B = 0.044715
 LANES = 128
+LIMIT = 4
 
 
 def up(value, unit):
@@ -61,6 +62,11 @@
 
 
 def tiles(total, step, body):
+    if total // step <= LIMIT:
+        for index in range(total // step):
+            body(index * step)
+        return
+
     @pl.loop(0, total // step)
     def _(index):
         body(pl.multiple_of(index * step, step))

time: 190 us -> 188 us (0.989)
  Pallas kernels: 189 us -> 187 us
    pallas_call x1, Pallas kernels: 180 us -> 178 us  [train(): pl.pallas_call(functools.partial(train_kernel, z), out_shape=(*[jax.Shape...]
where the time goes in v5:
time: 188 us
  Pallas kernels  187 us (99%)
    pallas_call x1, Pallas kernels, train(): pl.pallas_call(functools.partial(train_kernel, z), out_shape=(*[jax.Shape...  178 us
    pallas_call x1, Pallas kernels, update(): pl.pallas_call(functools.partial(update_kernel, z), out_shape=tuple(shape...  9.09 us

profile of v5, /device:TPU:0, one launch (start us, length us, event | category | flops | bytes accessed | tf_op | source)
XLA Modules:
  0.0 188.1 jit_solution(11875948726530911411)
XLA Ops:
  0.7 178.1 %train.1 = (f32[1280,128]{1,0:T(8,128)}, f32[1280,128]{1,0:T(8,128)}, f32[768,128]{1,0:T(8,128)}, f32[768,128]{1,0:T(8,128)}, f32[2,1024,256]{2,1,0:T(8,128)}, /*index=5*/f32[8,128]{1,0:T(8,128)}) custom-call(f32[602,512]{1,0:T(8,128)} %bitcast.25, f32[602,256]{1,0:T(8,128)} %bitcast.26, s32[4,256]{1,0:T(4,128)} %bitcast.36, s32[4,256]{1,0:T(4,128)} %bitcast.37, ...), custom_call_target="tpu_custom_call" | custom-call | tf_op jit(solution)/shard_map/train/pallas_call | solution.py:948
  178.8 9.1 %update.1 = (f32[1204,256]{1,0:T(8,128)}, f32[1204,256]{1,0:T(8,128)}, f32[1204,256]{1,0:T(8,128)}, bf16[1204,256]{1,0:T(8,128)(2,1)}, f32[512,256]{1,0:T(8,128)...) custom-call(f32[1280,128]{1,0:T(8,128)} %get-tuple-element.46.two_hb, ...), custom_call_target="tpu_custom_call" | custom-call | tf_op jit(solution)/shard_map/update/pallas_call | solution.py:1084

commit v6 on v5

--- a/solution.py
+++ b/solution.py
@@ -495,7 +495,7 @@
     pick(tb.at[1], send_b.at[1])
     sums[0].swap()
     sums[1].swap()
-    exchange_start(send_b.at[1], recv_b.at[1], 3, 0, 4)
+    exchange_start(send_b.at[1], recv_b.at[1], 3, 0, 6)
     put_pair(w2h, w2l, slice(0, 2 * hid), slice(0, hid), w2[...])
     w3t[...] = jnp.zeros(w3t.shape, F32)
     w3t[0 : z.cls, :] = w3[...]
@@ -503,7 +503,7 @@
     turn(ab, abt, z.rows, z.table)
     sums[0].gather()
     sums[1].gather()
-    exchange_start(send_b.at[1], recv_b.at[1], 3, 4, 8)
+    exchange_start(send_b.at[1], recv_b.at[1], 3, 6, 8)
     for grad in grads:
         grad.source[...] = jnp.zeros(grad.source.shape, F32)
 

time: 188 us -> 188 us (level)
  no operation moved by 1% of the time
where the time goes in v6:
time: 188 us; the launch traced here: 187 us
  Pallas kernels  187 us (99%)
    pallas_call x1, Pallas kernels, train(): pl.pallas_call(functools.partial(train_kernel, z), out_shape=(*[jax.Shape...  177 us
    pallas_call x1, Pallas kernels, update(): pl.pallas_call(functools.partial(update_kernel, z), out_shape=tuple(shape...  9.09 us

profile of v6, /device:TPU:0, one launch (start us, length us, event | category | flops | bytes accessed | tf_op | source)
XLA Modules:
  0.0 187.4 jit_solution(15896989470331162114)
XLA Ops:
  0.7 177.5 %train.1 = (f32[1280,128]{1,0:T(8,128)}, f32[1280,128]{1,0:T(8,128)}, f32[768,128]{1,0:T(8,128)}, f32[768,128]{1,0:T(8,128)}, f32[2,1024,256]{2,1,0:T(8,128)}, /*index=5*/f32[8,128]{1,0:T(8,128)}) custom-call(f32[602,512]{1,0:T(8,128)} %bitcast.25, f32[602,256]{1,0:T(8,128)} %bitcast.26, s32[4,256]{1,0:T(4,128)} %bitcast.36, s32[4,256]{1,0:T(4,128)} %bitcast.37, ...), custom_call_target="tpu_custom_call" | custom-call | tf_op jit(solution)/shard_map/train/pallas_call | solution.py:948
  178.1 9.1 %update.1 = (f32[1204,256]{1,0:T(8,128)}, f32[1204,256]{1,0:T(8,128)}, f32[1204,256]{1,0:T(8,128)}, bf16[1204,256]{1,0:T(8,128)(2,1)}, f32[512,256]{1,0:T(8,128)...) custom-call(f32[1280,128]{1,0:T(8,128)} %get-tuple-element.46.two_hb, ...), custom_call_target="tpu_custom_call" | custom-call | tf_op jit(solution)/shard_map/update/pallas_call | solution.py:1084
